TPU v7x, 1024 devices: a whole 8x8x8 slice. The times are simulated.
1024 devices in a mesh: dp: 128 (over z, x, core), tensor: 8 (over y).
Axes of the slice: x: 8, y: 8, z: 8, core: 2. Of those that a mesh axis runs over, the one named last changes fastest.
Arguments:
- saved_x: bfloat16 [65536, 5120], P('dp', 'tensor'), may hold values from -6 to 6
- grad_key: bfloat16 [65536, 1024], P('dp', 'tensor'), may hold values from -24 to 24
- w_key: bfloat16 [1024, 5120], P('dp', 'tensor'), may hold values from -0.1875 to 0.1875
- lengths: int32 [128], replicated, may hold values from 128 to 512, as said below
Outputs:
- grad_input: bfloat16 [65536, 5120], P('dp', 'tensor')
- grad_weight: float32 [1024, 5120], P('dp', 'tensor')
Inputs may be any that keep to these rules, and one draw needn't show every extreme that they name: `lengths`: each is a multiple of 128; group 0 is full and group 1 holds one block.
All inputs are finite; a program needn't handle non-finite values.
Results may differ from a plain program's by a relative error of at most 0.001.
Values may be sent and summed in bfloat16 or wider, within the bound.
No kernel may reach another device: no remote copies, remote signals or barrier semaphores. Data moves between devices by JAX's collectives and lax.ppermute only.
A program may use at most 32 MiB of HBM per device.

v0:
```python
import math

import jax
import jax.numpy as jnp
from jax import lax
from jax.sharding import PartitionSpec as P

BLOCK = 128


def per_device(saved_x, grad_key, w_key, lengths):
    rows = saved_x.shape[0]
    width = saved_x.shape[1]
    weights = lax.all_gather(w_key, "dp", axis=0, tiled=True)
    grads = lax.all_gather(grad_key, "tensor", axis=1, tiled=True)
    features = grads.shape[1]
    me_rank = lax.axis_index("dp")
    mine = lengths[me_rank] // BLOCK
    positions = jnp.arange(rows, dtype=jnp.int32)
    grads = jnp.where((positions < lengths[me_rank])[:, None], grads, jnp.zeros_like(grads))

    def run_block(step, carry):
        grad_rows, grad_sum = carry
        inputs = lax.dynamic_slice_in_dim(saved_x, step * BLOCK, BLOCK, 0)
        pieces = lax.dynamic_slice_in_dim(grads, step * BLOCK, BLOCK, 0)
        result = jnp.einsum("rk,kd->rd", pieces, weights, preferred_element_type=jnp.float32)
        grad_rows = lax.dynamic_update_slice_in_dim(
            grad_rows, result.astype(jnp.bfloat16), step * BLOCK, 0
        )
        grad_sum = grad_sum + jnp.einsum(
            "rk,rd->kd", pieces, inputs, preferred_element_type=jnp.float32
        )
        return (grad_rows, grad_sum)

    start_state = (
        jnp.zeros((rows, width), jnp.bfloat16),
        jnp.zeros((features, width), jnp.float32),
    )
    grad_rows, grad_sum = lax.fori_loop(0, mine, run_block, start_state)
    scale_factor = 1.0 / math.sqrt(rows * lax.axis_size("dp"))
    grad_weight = lax.psum_scatter(grad_sum * scale_factor, "dp", scatter_dimension=0, tiled=True)
    return (grad_rows, grad_weight)


def solution(mesh):
    placed = (P("dp", "tensor"), P("dp", "tensor"), P("dp", "tensor"), P())
    return jax.shard_map(
        per_device,
        mesh=mesh,
        in_specs=placed,
        out_specs=(P("dp", "tensor"), P("dp", "tensor")),
        check_vma=False,
    )
```

profile of v0, /device:TPU:1, one launch (start us, length us, event | category | flops | bytes accessed | tf_op | source)
XLA Modules:
  0.0 394.5 jit_solution(8359697761591047552)
XLA Ops:
  7.2 0.0 all-gather.3.cloned.1.call-start
  7.2 0.7 all-gather.3.cloned.1.call-update
  7.9 0.0 all-gather.5.cloned.1.call-start
  7.9 0.7 all-gather.5.cloned.1.call-update
  8.6 0.0 all-reduce.3.cloned.1.call-start
  8.7 1.2 dynamic_slice.10
  12.5 0.7 iota_compare_fusion
  13.2 50.2 %all-gather.3.cloned.1.call-done = bf16[512,1024]{1,0:T(8,128)(2,1)} async-done(((bf16[512,128]{1,0:T(8,128)(2,1)}), bf16[512,1024]{1,0:T(8,128)(2,1)}) %all-gather.3.cloned.1.call-update) | async-done | bytes 1048592 | tf_op jit(solution)/shard_map/all_gather | solution.py:15
  63.4 2.4 broadcast_select_fusion
  65.8 96.0 %all-gather.5.cloned.1.call-done = bf16[1024,640]{1,0:T(8,128)(2,1)} async-done(((bf16[8,640]{1,0:T(8,128)(2,1)}), bf16[1024,640]{1,0:T(8,128)(2,1)}) %all-gather.5.cloned.1.call-update) | async-done | bytes 1310736 | tf_op jit(solution)/shard_map/all_gather | solution.py:14
  161.8 0.2 broadcast_in_dim.19
  162.0 0.1 broadcast_in_dim.18
  162.0 3.2 while.12
  162.1 0.0 copy-start
  162.1 1.8 convolution_add_fusion.2
  163.9 0.0 copy-done
  163.9 1.4 fusion.16
  165.3 0.0 copy-start.1
  165.3 1.7 broadcast_multiply_fusion
  167.0 0.0 copy-done.1
  167.0 0.0 all-reduce.3.cloned.1.call-update
  167.0 1.3 dynamic-slice
  168.9 217.7 %all-reduce.3.cloned.1.call-done = f32[1024,640]{1,0:T(8,128)} async-done(((f32[1024,640]{1,0:T(8,128)}), f32[1024,640]{1,0:T(8,128)}) %all-reduce.3.cloned.1.call-update) | async-done | bytes 2621456
  386.7 1.3 constant_dynamic-slice_fusion
Async XLA Ops:
  7.2 56.3 %all-gather.3.cloned.1.call-start = ((), (), s32[]{:S(2)}) async-start(), calls=%async_computation | async-start | bytes 1179648 | tf_op jit(solution)/shard_map/all_gather | solution.py:15
  7.9 153.9 %all-gather.5.cloned.1.call-start = ((), (), s32[]{:S(2)}) async-start(), calls=%async_computation.1 | async-start | bytes 1320960 | tf_op jit(solution)/shard_map/all_gather | solution.py:14
  8.6 378.0 %all-reduce.3.cloned.1.call-start = ((), (), s32[]{:S(2)}) async-start(), calls=%async_computation.2 | async-start | bytes 5242880
  162.1 1.8 copy-start
  165.3 1.7 copy-start.1
Sparse Core Ops, SparseCore 0:
  10.6 52.8 all-gather.2
  67.8 93.9 all-gather.4
  167.1 219.4 all-reduce.2
where the time goes:
time: 397 us; the launch traced here: 395 us
  waiting for transfers between devices  365 us (92%)
  between operations  17 us (4%)
  other arithmetic  4.71 us (1%)
  local copies, waits for them, and re-layouts  4.09 us (1%)
    unnamed x4, waiting for transfers between devices  219 us
    all_gather x1, waiting for transfers between devices, per_device(): weights = lax.all_gather(w_key, 'dp', axis=0, tiled=True)  96 us
    all_gather x1, waiting for transfers between devices, per_device(): grads = lax.all_gather(grad_key, 'tensor', axis=1, tiled=True)  50.2 us
  transfers between devices with their start and end apart: 3, of which 3 were waited for; matrix products, arithmetic and copies ran while one was open for 1% of the time, Pallas kernels for 0%

commit v1 on v0

v1 whole, which is shorter than its diff:
```python
import functools
import math

import jax
import jax.numpy as jnp
from jax import lax
from jax.experimental import pallas as pl
from jax.experimental.pallas import tpu as pltpu
from jax.sharding import Mesh, PartitionSpec as P

STEPS = 256.0
LARGEST = 32767.0
VMEM = pl.BlockSpec(memory_space=pltpu.VMEM)


def grads_kernel(g_ref, x_ref, own_ref, oth_ref):
    half = own_ref.shape[1]

    def block(k, _):
        d = lax.dot_general(g_ref[k], x_ref[...], (((0,), (0,)), ((), ())), preferred_element_type=jnp.float32)
        oth_ref[k] = d[half:]
        own_ref[k] = d[:half]
        return 0

    lax.fori_loop(0, g_ref.shape[0], block, 0)


def input_kernel(g_ref, own_ref, oth_ref, out_ref, w_ref):
    blocks, rows, width = g_ref.shape
    half = width // 2
    for k in range(blocks):
        w_ref[k * width : k * width + half, :] = own_ref[k * half : (k + 1) * half, :]
        w_ref[k * width + half : (k + 1) * width, :] = oth_ref[k * half : (k + 1) * half, :]
    part = min(rows, 128)

    def run(i, _):
        at = pl.ds(pl.multiple_of(i * part, part), part)
        g = jnp.concatenate([g_ref[k, at, :] for k in range(blocks)], axis=1)
        out_ref[at, :] = jnp.dot(g, w_ref[...], preferred_element_type=jnp.float32).astype(out_ref.dtype)
        return 0

    lax.fori_loop(0, rows // part, run, 0)


def pack_kernel(a_ref, b_ref, out_ref):
    width = a_ref.shape[2]
    lanes = out_ref.shape[2] - width

    def run(k, _):
        v = a_ref[k] + b_ref[k]
        top = jnp.maximum(jnp.max(jnp.abs(v), axis=1, keepdims=True), 1e-30)
        e = jnp.ceil(STEPS * jnp.log2(top * (1.0 / LARGEST))) + 1.0
        q = jnp.round(v * jnp.exp2(e * (-1.0 / STEPS)))
        out_ref[k, :, :width] = q.astype(jnp.int32).astype(jnp.int16)
        out_ref[k, :, width:] = jnp.broadcast_to(e, (v.shape[0], lanes)).astype(jnp.int32).astype(jnp.int16)
        return 0

    lax.fori_loop(0, a_ref.shape[0], run, 0)


def sum_kernel(scale, in_ref, out_ref):
    sources, rows, whole = in_ref.shape
    width = out_ref.shape[1]
    lanes = whole - width
    out_ref[...] = jnp.zeros_like(out_ref)
    part = min(8, sources)

    def run(k, _):
        total = [jnp.zeros((rows, lanes), jnp.float32) for _ in range(width // lanes)]
        for j in range(part):
            s = k * part + j
            step = jnp.exp2(in_ref[s, :, width:].astype(jnp.int32).astype(jnp.float32) * (1.0 / STEPS))
            for t in range(width // lanes):
                q = in_ref[s, :, t * lanes : (t + 1) * lanes].astype(jnp.int32).astype(jnp.float32)
                total[t] = total[t] + q * step
        for t in range(width // lanes):
            out_ref[:, t * lanes : (t + 1) * lanes] += total[t] * scale
        return 0

    lax.fori_loop(0, sources // part, run, 0)


def call(kernel, shapes, n, name, scratch=(), flops=0, moved=0):
    return pl.pallas_call(
        kernel,
        out_shape=shapes,
        in_specs=[VMEM] * n,
        out_specs=[VMEM] * len(shapes) if isinstance(shapes, (list, tuple)) else VMEM,
        scratch_shapes=scratch,
        compiler_params=pltpu.CompilerParams(vmem_limit_bytes=12 * 1024 * 1024),
        cost_estimate=pl.CostEstimate(flops=flops, bytes_accessed=moved, transcendentals=0),
        name=name,
    )


def merge_kernel(upper_ref, held_ref, got_ref, out_ref):
    upper = upper_ref[0]
    out_ref[:, pl.ds(upper, 1)] = held_ref[...][:, None]
    out_ref[:, pl.ds(1 - upper, 1)] = got_ref[...][:, None]


def double(held, axis, size, distances):
    for far in distances:
        got = lax.ppermute(held, axis, [(i, i ^ far) for i in range(size)])
        upper = (lax.axis_index(axis) // far) % 2
        count, rows, width = held.shape
        held = pl.pallas_call(
            merge_kernel,
            out_shape=jax.ShapeDtypeStruct((count, 2, rows, width), held.dtype),
            in_specs=[pl.BlockSpec(memory_space=pltpu.SMEM), VMEM, VMEM],
            out_specs=VMEM,
            compiler_params=pltpu.CompilerParams(vmem_limit_bytes=4 * 1024 * 1024),
            name="merge",
        )(upper.astype(jnp.int32).reshape(1), held, got).reshape(2 * count, rows, width)
    return held


def per_device(nz, nx, ny, x, g, w, lengths):
    rows, width = x.shape
    block = g.shape[1]
    half = block // 2
    core = lax.axis_index("c")
    group = (lax.axis_index("z") * nx + lax.axis_index("x")) * 2 + core

    x_steps = [nx >> i for i in range(1, nx.bit_length())]
    own = double(w[None], "z", nz, [nz >> i for i in range(1, nz.bit_length())])
    own = double(own, "x", nx, x_steps[:-2])

    live = jnp.arange(rows, dtype=jnp.int32) < lengths[group]
    masked = jnp.where(live[:, None], g, jnp.zeros_like(g))
    place = jnp.arange(block, dtype=jnp.int32)
    inner = place % half
    source = (inner // 8) * 16 + inner % 8 + 8 * jnp.where(place < half, core, 1 - core)
    order = (place[:, None] == source[None, :]).astype(g.dtype)
    sorted_g = jnp.dot(masked, order, preferred_element_type=jnp.float32).astype(g.dtype)
    grads = lax.all_to_all(jnp.broadcast_to(sorted_g[None], (ny,) + g.shape), "tensor", 0, 0)

    grads, own = lax.optimization_barrier((grads, own))
    own = double(own, "x", nx, x_steps[-2:-1])

    other_core = [(0, 1), (1, 0)]

    f32 = jax.ShapeDtypeStruct((ny, half, width), jnp.float32)
    mine, others = call(
        grads_kernel, (f32, f32), 2, "weight_grads", flops=2 * rows * ny * block * width, moved=6_000_000
    )(grads, x)
    got = lax.ppermute(others, "c", other_core)

    lanes = min(128, width)
    code = call(
        pack_kernel,
        jax.ShapeDtypeStruct((ny, half, width + lanes), jnp.int16),
        2,
        "pack",
        moved=4_000_000,
    )(mine, got)
    code, own = lax.optimization_barrier((code, own))
    code = lax.all_to_all(code.reshape(nz * nx, 8, width + lanes), ("z", "x"), 0, 0)
    scale = 1.0 / math.sqrt(rows * nz * nx * 2)
    grad_weight = call(
        functools.partial(sum_kernel, scale), jax.ShapeDtypeStruct((8, width), jnp.float32), 1, "unpack_sum", moved=1_000_000
    )(code)

    own = double(own, "x", nx, x_steps[-1:]).reshape(nz * half, width)
    oth = lax.ppermute(own, "c", other_core)
    grad_input = call(
        input_kernel,
        jax.ShapeDtypeStruct((rows, width), jnp.bfloat16),
        3,
        "input_grads",
        scratch=[pltpu.VMEM((ny * block, width), jnp.bfloat16)],
        flops=2 * rows * ny * block * width,
        moved=6_000_000,
    )(grads, own, oth)
    return (grad_input, grad_weight)


def solution(mesh):
    dp, ny = mesh.shape["dp"], mesh.shape["tensor"]
    nz, nx = ny, dp // (2 * ny)
    fine = Mesh(mesh.devices.reshape(nz, nx, 2, ny), ("z", "x", "c", "tensor"))
    both = P(("z", "x", "c"), "tensor")
    return jax.shard_map(
        functools.partial(per_device, nz, nx, ny),
        mesh=fine,
        in_specs=(both, both, both, P()),
        out_specs=(both, both),
        check_vma=False,
    )
```

time: 397 us -> 124 us (0.31)
  waiting for transfers between devices: 365 us -> 37.4 us
  starting transfers between devices: 0.11 us -> 71.3 us
  between operations: 17 us -> 0.92 us
  Pallas kernels: 0 us -> 10 us
  other arithmetic: 4.71 us -> 0.66 us
    unnamed x4 -> x0, waiting for transfers between devices: 219 us -> none
    all_gather x2 -> x0, waiting for transfers between devices: 146 us -> none  [the longest x1 96 us: per_device(): weights = lax.all_gather(w_key, 'dp', axis=0, tiled=True)]
    ppermute x0 -> x8, starting transfers between devices: none -> 48.7 us  [the longest x6 38.6 us: double(): got = lax.ppermute(held, axis, [(i, i ^ far) for i in range(size)])]
    ppermute x0 -> x8, waiting for transfers between devices: none -> 37.4 us  [the longest x6 35.7 us: double(): got = lax.ppermute(held, axis, [(i, i ^ far) for i in range(size)])]
    all_to_all x0 -> x2, starting transfers between devices: none -> 22.7 us  [the longest x1 14.4 us: per_device(): lax.all_to_all(code.reshape(nz * nx, 8, width + lanes), ('z', 'x'), 0, 0)]
    pallas_call x0 -> x10, Pallas kernels: none -> 10 us  [the longest x1 3.4 us: per_device(): call(grads_kernel, (f32, f32), 2, 'weight_grads', flops=2 * rows * ny * b...]
  transfers between devices with their start and end apart: 3 -> 10, of which waited for: 3 -> 7; matrix products, arithmetic and copies ran while one was open for 1% -> 0% of each run, Pallas kernels for 0% -> 2%
where the time goes in v1:
time: 124 us
  starting transfers between devices  71.3 us (58%)
  waiting for transfers between devices  37.4 us (30%)
  Pallas kernels  10 us (8%)
  local copies, waits for them, and re-layouts  2.37 us (2%)
    ppermute x6, starting transfers between devices, double(): got = lax.ppermute(held, axis, [(i, i ^ far) for i in range(size)])  38.6 us
    ppermute x6, waiting for transfers between devices, double(): got = lax.ppermute(held, axis, [(i, i ^ far) for i in range(size)])  35.7 us
    all_to_all x1, starting transfers between devices, per_device(): lax.all_to_all(code.reshape(nz * nx, 8, width + lanes), ('z', 'x'), 0, 0)  14.4 us
    all_to_all x1, starting transfers between devices, per_device(): lax.all_to_all(jnp.broadcast_to(sorted_g[None], (ny,) + g.shape), 'tensor...  8.24 us
    ppermute x1, starting transfers between devices, per_device(): got = lax.ppermute(others, 'c', other_core)  6.66 us
    ppermute x1, starting transfers between devices, per_device(): oth = lax.ppermute(own, 'c', other_core)  3.46 us
    pallas_call x1, Pallas kernels, per_device(): call(grads_kernel, (f32, f32), 2, 'weight_grads', flops=2 * rows * ny * b...  3.4 us
    pallas_call x1, Pallas kernels, per_device(): call(pack_kernel, jax.ShapeDtypeStruct((ny, half, width + lanes), jnp.int...  3.17 us
  transfers between devices with their start and end apart: 10, of which 7 were waited for; matrix products, arithmetic and copies ran while one was open for 0% of the time, Pallas kernels for 2%

profile of v1, /device:TPU:1, one launch (start us, length us, event | category | flops | bytes accessed | tf_op | source)
XLA Modules:
  0.0 123.9 jit_solution(14874404115527373132)
XLA Ops:
  0.6 1.2 %dynamic_slice.3 = s32[1]{0:T(128)} dynamic-slice(s32[128]{0:T(128)} %param.7, s32[]{:T(128)S(6)} %select_n.84), dynamic_slice_sizes={1} | dynamic-slice | bytes 12 | tf_op jit(solution)/shard_map/dynamic_slice | solution.py:129
  1.9 0.6 iota_compare_fusion.2
  2.6 1.2 convolution_convert_fusion
  3.7 1.1 broadcast_in_dim.35
  4.8 0.0 copy-start
  4.8 0.0 copy-start.1
  4.8 8.2 %all-to-all-start = ((bf16[8,512,128]{2,1,0:T(8,128)(2,1)}), bf16[8,512,128]{2,1,0:T(8,128)(2,1)S(1)}, u32[]{:S(2)}, u32[]{:S(2)}) async-start(bf16[8,512,128]{2,1,0:T(8,128)(2,1)} %broadcast_in_dim.35), calls=%async_computation | async-start | bytes 2097152 | tf_op jit(solution)/shard_map/all_to_all | solution.py:136
  13.1 0.0 copy-done
  13.1 14.3 %collective-permute-start = (bf16[1,8,640]{2,1,0:T(8,128)(2,1)S(1)}, bf16[1,8,640]{2,1,0:T(8,128)(2,1)S(1)}, u32[]{:S(2)}, u32[]{:S(2)}) collective-permute-start(bf16[1,8,640]{2,1,0:T(8,128)(2,1)S(1)} %bitcast.27), channel_id=1, source_target_pairs={{0,512},{128,640},{256,768},{384,896},{512,0},{640,128},{768,256},... | collective-permute-start | bytes 30728 | tf_op jit(solution)/shard_map/ppermute | solution.py:104
  27.4 1.0 collective-permute-done.got_ref
  28.4 5.8 %collective-permute-start.1 = (bf16[2,8,640]{2,1,0:T(8,128)(2,1)S(1)}, bf16[2,8,640]{2,1,0:T(8,128)(2,1)S(1)}, u32[]{:S(2)}, u32[]{:S(2)}) collective-permute-start(bf16[2,8,640]{2,1,0:T(8,128)(2,1)S(1)} %bitcast.25), channel_id=1, source_target_pairs={{0,256},{128,384},{256,0},{384,128},{512,768},{640,896},{768,512},... | collective-permute-start | bytes 61448 | tf_op jit(solution)/shard_map/ppermute | solution.py:104
  34.3 1.2 collective-permute-done.1.got_ref
  35.5 4.2 %collective-permute-start.2 = (bf16[4,8,640]{2,1,0:T(8,128)(2,1)S(1)}, bf16[4,8,640]{2,1,0:T(8,128)(2,1)S(1)}, u32[]{:S(2)}, u32[]{:S(2)}) collective-permute-start(bf16[4,8,640]{2,1,0:T(8,128)(2,1)S(1)} %bitcast.23), channel_id=1, source_target_pairs={{0,128},{128,0},{256,384},{384,256},{512,640},{640,512},{768,896},... | collective-permute-start | bytes 122888 | tf_op jit(solution)/shard_map/ppermute | solution.py:104
  39.7 1.7 %collective-permute-done.2.got_ref = bf16[4,8,640]{2,1,0:T(8,128)(2,1)S(1)} collective-permute-done((bf16[4,8,640]{2,1,0:T(8,128)(2,1)S(1)}, bf16[4,8,640]{2,1,0:T(8,128)(2,1)S(1)}, u32[]{:S(2)}, u32[]{:S(2)}) %collective-permute-start.2) | collective-permute-done | bytes 40992 | tf_op jit(solution)/shard_map/ppermute | solution.py:104
  41.4 7.1 %collective-permute-start.3 = (bf16[8,8,640]{2,1,0:T(8,128)(2,1)S(1)}, bf16[8,8,640]{2,1,0:T(8,128)(2,1)S(1)}, u32[]{:S(2)}, u32[]{:S(2)}) collective-permute-start(bf16[8,8,640]{2,1,0:T(8,128)(2,1)S(1)} %bitcast.21), channel_id=1, source_target_pairs={{0,64},{16,80},{32,96},{48,112},{64,0},{80,16},{96,32},{112,48},{1... | collective-permute-start | bytes 245768 | tf_op jit(solution)/shard_map/ppermute | solution.py:104
  48.5 2.0 %collective-permute-done.3.got_ref = bf16[8,8,640]{2,1,0:T(8,128)(2,1)S(1)} collective-permute-done((bf16[8,8,640]{2,1,0:T(8,128)(2,1)S(1)}, bf16[8,8,640]{2,1,0:T(8,128)(2,1)S(1)}, u32[]{:S(2)}, u32[]{:S(2)}) %collective-permute-start.3) | collective-permute-done | bytes 81952 | tf_op jit(solution)/shard_map/ppermute | solution.py:104
  50.6 0.0 all-to-all-done.g_ref
  50.6 0.0 copy-done.1
  50.6 3.4 %weight_grads.1 = (f32[8,64,640]{2,1,0:T(8,128)S(1)}, f32[8,64,640]{2,1,0:T(8,128)}) custom-call(bf16[8,512,128]{2,1,0:T(8,128)(2,1)S(1)} %all-to-all-done.g_ref, bf16[512,640]{1,0:T(8,128)(2,1)S(1)} %copy-done.1), custom_call_target="tpu_custom_call" | custom-call | flops 671088640 | bytes 6000000 | tf_op jit(solution)/shard_map/weight_grads/pallas_call | solution.py:144
  54.0 6.7 %collective-permute-start.4 = (f32[8,64,640]{2,1,0:T(8,128)}, f32[8,64,640]{2,1,0:T(8,128)}, u32[]{:S(2)}, u32[]{:S(2)}) collective-permute-start(f32[8,64,640]{2,1,0:T(8,128)} %get-tuple-element.10), channel_id=1, source_target_pairs={{0,8},{8,0},{1,9},{9,1},{2,10},{10,2},{3,11},{11,3},{4,12},{12,4},... | collective-permute-start | bytes 3932168 | tf_op jit(solution)/shard_map/ppermute | solution.py:147
  60.7 4.2 %collective-permute-start.5 = (bf16[16,8,640]{2,1,0:T(8,128)(2,1)S(1)}, bf16[16,8,640]{2,1,0:T(8,128)(2,1)S(1)}, u32[]{:S(2)}, u32[]{:S(2)}) collective-permute-start(bf16[16,8,640]{2,1,0:T(8,128)(2,1)S(1)} %bitcast.19), channel_id=1, source_target_pairs={{0,32},{16,48},{32,0},{48,16},{64,96},{80,112},{96,64},{112,80},{1... | collective-permute-start | bytes 491528 | tf_op jit(solution)/shard_map/ppermute | solution.py:104
  64.9 7.9 %collective-permute-done.5.got_ref = bf16[16,8,640]{2,1,0:T(8,128)(2,1)S(1)} collective-permute-done((bf16[16,8,640]{2,1,0:T(8,128)(2,1)S(1)}, bf16[16,8,640]{2,1,0:T(8,128)(2,1)S(1)}, u32[]{:S(2)}, u32[]{:S(2)}) %collective-permute-start.5) | collective-permute-done | bytes 163872 | tf_op jit(solution)/shard_map/ppermute | solution.py:104
  72.9 0.0 collective-permute-done.4.b_ref
  72.9 3.2 %pack.1 = s16[8,64,768]{2,1,0:T(8,128)(2,1)} custom-call(f32[8,64,640]{2,1,0:T(8,128)S(1)} %get-tuple-element.9.a_ref, f32[8,64,640]{2,1,0:T(8,128)} %collective-permute-done.4.b_ref), custom_call_target="tpu_custom_call" | custom-call | bytes 4000000 | tf_op jit(solution)/shard_map/pack/pallas_call | solution.py:150
  76.0 14.4 %all-to-all-start.1 = ((s16[64,8,768]{2,1,0:T(8,128)(2,1)}), s16[64,8,768]{2,1,0:T(8,128)(2,1)S(1)}, u32[]{:S(2)}, u32[]{:S(2)}) async-start(s16[64,8,768]{2,1,0:T(8,128)(2,1)} %bitcast.14), calls=%async_computation.1 | async-start | bytes 1572864 | tf_op jit(solution)/shard_map/all_to_all | solution.py:158
  90.5 2.9 %collective-permute-start.6 = (bf16[32,8,640]{2,1,0:T(8,128)(2,1)S(1)}, bf16[32,8,640]{2,1,0:T(8,128)(2,1)S(1)}, u32[]{:S(2)}, u32[]{:S(2)}) collective-permute-start(bf16[32,8,640]{2,1,0:T(8,128)(2,1)S(1)} %bitcast.17), channel_id=1, source_target_pairs={{0,16},{16,0},{32,48},{48,32},{64,80},{80,64},{96,112},{112,96},{1... | collective-permute-start | bytes 983048 | tf_op jit(solution)/shard_map/ppermute | solution.py:104
  93.4 21.9 %collective-permute-done.6.got_ref = bf16[32,8,640]{2,1,0:T(8,128)(2,1)S(1)} collective-permute-done((bf16[32,8,640]{2,1,0:T(8,128)(2,1)S(1)}, bf16[32,8,640]{2,1,0:T(8,128)(2,1)S(1)}, u32[]{:S(2)}, u32[]{:S(2)}) %collective-permute-start.6) | collective-permute-done | bytes 327712 | tf_op jit(solution)/shard_map/ppermute | solution.py:104
  115.3 0.1 merge.11
  115.3 3.5 %collective-permute-start.7 = (bf16[512,640]{1,0:T(8,128)(2,1)S(1)}, bf16[512,640]{1,0:T(8,128)(2,1)S(1)}, u32[]{:S(2)}, u32[]{:S(2)}) collective-permute-start(bf16[512,640]{1,0:T(8,128)(2,1)S(1)} %bitcast.15), channel_id=1, source_target_pairs={{0,8},{8,0},{1,9},{9,1},{2,10},{10,2},{3,11},{11,3},{4,12},{12,4},... | collective-permute-start | bytes 1966088 | tf_op jit(solution)/shard_map/ppermute | solution.py:165
  118.8 1.7 %collective-permute-done.7.oth_ref = bf16[512,640]{1,0:T(8,128)(2,1)S(1)} collective-permute-done((bf16[512,640]{1,0:T(8,128)(2,1)S(1)}, bf16[512,640]{1,0:T(8,128)(2,1)S(1)}, u32[]{:S(2)}, u32[]{:S(2)}) %collective-permute-start.7) | collective-permute-done | bytes 655392 | tf_op jit(solution)/shard_map/ppermute | solution.py:165
  120.5 2.5 %input_grads.1 = bf16[512,640]{1,0:T(8,128)(2,1)} custom-call(bf16[8,512,128]{2,1,0:T(8,128)(2,1)S(1)} %all-to-all-done.g_ref, bf16[512,640]{1,0:T(8,128)(2,1)S(1)} %bitcast.16, bf16[512,640]{1,0:T(8,128)(2,1)S(1)} %collective-permute-done.7.oth_ref), custom_call_target="tpu_custom_call" | custom-call | flops 671088640 | bytes 6000000 | tf_op jit(solution)/shard_map/input_grads/pallas_call | solution.py:166
  123.0 0.0 all-to-all-done.1.in_ref
  123.0 0.9 unpack_sum.1
  (6 shorter events, 0.1 us)
Async XLA Ops:
  4.8 8.2 %copy-start = (bf16[8,640]{1,0:T(8,128)(2,1)S(1)}, bf16[8,640]{1,0:T(8,128)(2,1)}, u32[]{:S(2)}) copy-start(bf16[8,640]{1,0:T(8,128)(2,1)} %param.6) | copy-start | bytes 30724
  4.8 45.8 %copy-start.1 = (bf16[512,640]{1,0:T(8,128)(2,1)S(1)}, bf16[512,640]{1,0:T(8,128)(2,1)}, u32[]{:S(2)}) copy-start(bf16[512,640]{1,0:T(8,128)(2,1)} %x_ref.1) | copy-start | bytes 1966084
  4.8 45.8 %all-to-all-start = ((bf16[8,512,128]{2,1,0:T(8,128)(2,1)}), bf16[8,512,128]{2,1,0:T(8,128)(2,1)S(1)}, u32[]{:S(2)}, u32[]{:S(2)}) async-start(bf16[8,512,128]{2,1,0:T(8,128)(2,1)} %broadcast_in_dim.35), calls=%async_computation | async-start | bytes 2097152 | tf_op jit(solution)/shard_map/all_to_all | solution.py:136
  13.1 15.3 %collective-permute-start = (bf16[1,8,640]{2,1,0:T(8,128)(2,1)S(1)}, bf16[1,8,640]{2,1,0:T(8,128)(2,1)S(1)}, u32[]{:S(2)}, u32[]{:S(2)}) collective-permute-start(bf16[1,8,640]{2,1,0:T(8,128)(2,1)S(1)} %bitcast.27), channel_id=1, source_target_pairs={{0,512},{128,640},{256,768},{384,896},{512,0},{640,128},{768,256},... | collective-permute-start | bytes 30728 | tf_op jit(solution)/shard_map/ppermute | solution.py:104
  28.4 7.0 %collective-permute-start.1 = (bf16[2,8,640]{2,1,0:T(8,128)(2,1)S(1)}, bf16[2,8,640]{2,1,0:T(8,128)(2,1)S(1)}, u32[]{:S(2)}, u32[]{:S(2)}) collective-permute-start(bf16[2,8,640]{2,1,0:T(8,128)(2,1)S(1)} %bitcast.25), channel_id=1, source_target_pairs={{0,256},{128,384},{256,0},{384,128},{512,768},{640,896},{768,512},... | collective-permute-start | bytes 61448 | tf_op jit(solution)/shard_map/ppermute | solution.py:104
  35.5 5.9 %collective-permute-start.2 = (bf16[4,8,640]{2,1,0:T(8,128)(2,1)S(1)}, bf16[4,8,640]{2,1,0:T(8,128)(2,1)S(1)}, u32[]{:S(2)}, u32[]{:S(2)}) collective-permute-start(bf16[4,8,640]{2,1,0:T(8,128)(2,1)S(1)} %bitcast.23), channel_id=1, source_target_pairs={{0,128},{128,0},{256,384},{384,256},{512,640},{640,512},{768,896},... | collective-permute-start | bytes 122888 | tf_op jit(solution)/shard_map/ppermute | solution.py:104
  41.4 9.2 %collective-permute-start.3 = (bf16[8,8,640]{2,1,0:T(8,128)(2,1)S(1)}, bf16[8,8,640]{2,1,0:T(8,128)(2,1)S(1)}, u32[]{:S(2)}, u32[]{:S(2)}) collective-permute-start(bf16[8,8,640]{2,1,0:T(8,128)(2,1)S(1)} %bitcast.21), channel_id=1, source_target_pairs={{0,64},{16,80},{32,96},{48,112},{64,0},{80,16},{96,32},{112,48},{1... | collective-permute-start | bytes 245768 | tf_op jit(solution)/shard_map/ppermute | solution.py:104
  54.0 18.8 %collective-permute-start.4 = (f32[8,64,640]{2,1,0:T(8,128)}, f32[8,64,640]{2,1,0:T(8,128)}, u32[]{:S(2)}, u32[]{:S(2)}) collective-permute-start(f32[8,64,640]{2,1,0:T(8,128)} %get-tuple-element.10), channel_id=1, source_target_pairs={{0,8},{8,0},{1,9},{9,1},{2,10},{10,2},{3,11},{11,3},{4,12},{12,4},... | collective-permute-start | bytes 3932168 | tf_op jit(solution)/shard_map/ppermute | solution.py:147
  60.7 12.1 %collective-permute-start.5 = (bf16[16,8,640]{2,1,0:T(8,128)(2,1)S(1)}, bf16[16,8,640]{2,1,0:T(8,128)(2,1)S(1)}, u32[]{:S(2)}, u32[]{:S(2)}) collective-permute-start(bf16[16,8,640]{2,1,0:T(8,128)(2,1)S(1)} %bitcast.19), channel_id=1, source_target_pairs={{0,32},{16,48},{32,0},{48,16},{64,96},{80,112},{96,64},{112,80},{1... | collective-permute-start | bytes 491528 | tf_op jit(solution)/shard_map/ppermute | solution.py:104
  76.0 47.0 %all-to-all-start.1 = ((s16[64,8,768]{2,1,0:T(8,128)(2,1)}), s16[64,8,768]{2,1,0:T(8,128)(2,1)S(1)}, u32[]{:S(2)}, u32[]{:S(2)}) async-start(s16[64,8,768]{2,1,0:T(8,128)(2,1)} %bitcast.14), calls=%async_computation.1 | async-start | bytes 1572864 | tf_op jit(solution)/shard_map/all_to_all | solution.py:158
  90.5 24.8 %collective-permute-start.6 = (bf16[32,8,640]{2,1,0:T(8,128)(2,1)S(1)}, bf16[32,8,640]{2,1,0:T(8,128)(2,1)S(1)}, u32[]{:S(2)}, u32[]{:S(2)}) collective-permute-start(bf16[32,8,640]{2,1,0:T(8,128)(2,1)S(1)} %bitcast.17), channel_id=1, source_target_pairs={{0,16},{16,0},{32,48},{48,32},{64,80},{80,64},{96,112},{112,96},{1... | collective-permute-start | bytes 983048 | tf_op jit(solution)/shard_map/ppermute | solution.py:104
  115.3 5.2 %collective-permute-start.7 = (bf16[512,640]{1,0:T(8,128)(2,1)S(1)}, bf16[512,640]{1,0:T(8,128)(2,1)S(1)}, u32[]{:S(2)}, u32[]{:S(2)}) collective-permute-start(bf16[512,640]{1,0:T(8,128)(2,1)S(1)} %bitcast.15), channel_id=1, source_target_pairs={{0,8},{8,0},{1,9},{9,1},{2,10},{10,2},{3,11},{11,3},{4,12},{12,4},... | collective-permute-start | bytes 1966088 | tf_op jit(solution)/shard_map/ppermute | solution.py:165

commit v2 on v0

v2 whole, which is shorter than its diff:
```python
import functools
import math

import jax
import jax.numpy as jnp
from jax import lax
from jax.experimental import pallas as pl
from jax.experimental.pallas import tpu as pltpu
from jax.sharding import Mesh, PartitionSpec as P

STEPS = 256.0
LARGEST = 32767.0
BIAS = 127.0
VMEM = pl.BlockSpec(memory_space=pltpu.VMEM)
SMEM = pl.BlockSpec(memory_space=pltpu.SMEM)


def sort_kernel(lengths_ref, place_ref, g_ref, out_ref):
    rows, width = g_ref.shape
    half = width // 2
    core = place_ref[0] % 2
    length = lengths_ref[place_ref[0]]
    take = lax.broadcasted_iota(jnp.int32, (width, width), 0)
    place = lax.broadcasted_iota(jnp.int32, (width, width), 1)
    inner = place % half
    kind = jnp.where(place < half, core, 1 - core)
    order = jnp.where(take == (inner // 8) * 16 + inner % 8 + 8 * kind, 1.0, 0.0).astype(g_ref.dtype)
    g = jnp.dot(g_ref[...], order, preferred_element_type=jnp.float32)
    live = lax.broadcasted_iota(jnp.int32, (rows, width), 0) < length
    g = jnp.where(live, g, 0.0).astype(out_ref.dtype)
    for k in range(out_ref.shape[0]):
        out_ref[k] = g


def other_kernel(g_ref, x_ref, oth_ref, own_ref, turned_ref):
    blocks, rows, width = g_ref.shape
    half = width // 2
    for k in range(blocks):
        turned = g_ref[k].T
        own_ref[k * half : (k + 1) * half, :] = turned[:half]
        turned_ref[k * half : (k + 1) * half, :] = turned[half:]
    oth_ref[...] = jnp.dot(turned_ref[...], x_ref[...], preferred_element_type=jnp.float32)


def own_kernel(g_ref, x_ref, out_ref):
    out_ref[...] = jnp.dot(g_ref[...], x_ref[...], preferred_element_type=jnp.float32)


def pack_kernel(a_ref, b_ref, w_ref, out_ref):
    rows, width = w_ref.shape
    lanes = out_ref.shape[2] - 2 * width

    def store(k, at, v):
        out_ref[k, :, at : at + v.shape[1]] = v.astype(jnp.int32).astype(out_ref.dtype)

    w = w_ref[...].astype(jnp.float32)
    size = jnp.abs(w)
    e = jnp.floor(jnp.log2(jnp.maximum(size, 2.0**-126)))
    bits = (e + BIAS) * 128.0 + (size * jnp.exp2(-e) * 128.0 - 128.0)
    bits = jnp.where(size < 2.0**-126, 0.0, bits)
    bits = jnp.round(jnp.where(w < 0.0, -bits, bits))
    for k in range(out_ref.shape[0]):
        v = a_ref[k] + b_ref[k]
        top = jnp.maximum(jnp.max(jnp.abs(v), axis=1, keepdims=True), 1e-30)
        e = jnp.ceil(STEPS * jnp.log2(top * (1.0 / LARGEST))) + 1.0
        store(k, 0, jnp.round(v * jnp.exp2(e * (-1.0 / STEPS))))
        store(k, width, jnp.broadcast_to(e, (rows, lanes)))
        store(k, width + lanes, bits)


def weights_kernel(in_ref, out_ref):
    width = out_ref.shape[2]
    for s in range(in_ref.shape[0]):
        bits = in_ref[s, :, in_ref.shape[2] - width :].astype(jnp.int32)
        size = jnp.abs(bits)
        e = (size >> 7).astype(jnp.float32) - BIAS
        v = ((size & 127) + 128).astype(jnp.float32) * jnp.exp2(e) * (1.0 / 128.0)
        v = jnp.where(size < 128, 0.0, jnp.where(bits < 0, -v, v))
        out_ref[s] = v.astype(out_ref.dtype)


def sum_kernel(scale, in_ref, out_ref):
    rows, width = out_ref.shape
    lanes = in_ref.shape[2] - 2 * width
    total = [jnp.zeros((rows, lanes), jnp.float32) for _ in range(width // lanes)]
    for s in range(in_ref.shape[0]):
        step = jnp.exp2(in_ref[s, :, width : width + lanes].astype(jnp.int32).astype(jnp.float32) * (1.0 / STEPS))
        for t in range(width // lanes):
            q = in_ref[s, :, t * lanes : (t + 1) * lanes].astype(jnp.int32).astype(jnp.float32)
            total[t] = total[t] + q * step
    for t in range(width // lanes):
        out_ref[:, t * lanes : (t + 1) * lanes] = total[t] * scale


def input_kernel(g_ref, own_ref, oth_ref, out_ref, w_ref):
    blocks, rows, width = g_ref.shape
    half = width // 2
    for k in range(blocks):
        w_ref[k * width : k * width + half, :] = own_ref[k * half : (k + 1) * half, :]
        w_ref[k * width + half : (k + 1) * width, :] = oth_ref[k * half : (k + 1) * half, :]
    g = jnp.concatenate([g_ref[k] for k in range(blocks)], axis=1)
    out_ref[...] = jnp.dot(g, w_ref[...], preferred_element_type=jnp.float32).astype(out_ref.dtype)


def call(kernel, out, specs, name, scratch=(), flops=0, moved=0):
    return pl.pallas_call(
        kernel,
        out_shape=[jax.ShapeDtypeStruct(*o) for o in out],
        in_specs=specs,
        out_specs=[VMEM] * len(out),
        scratch_shapes=scratch,
        compiler_params=pltpu.CompilerParams(vmem_limit_bytes=14 * 1024 * 1024),
        cost_estimate=pl.CostEstimate(flops=flops, bytes_accessed=moved, transcendentals=0),
        name=name,
    )


def per_device(nz, nx, ny, x, g, w, lengths):
    rows, width = x.shape
    block = g.shape[1]
    half = block // 2
    features = ny * half
    lanes = 128
    work = 2 * rows * features * width
    group = (lax.axis_index("z") * nx + lax.axis_index("x")) * 2 + lax.axis_index("c")
    swap = [(0, 1), (1, 0)]

    (copies,) = call(sort_kernel, [((ny, rows, block), g.dtype)], [SMEM, SMEM, VMEM], "sort", moved=2_000_000)(
        lengths, group.astype(jnp.int32).reshape(1), g
    )
    grads = lax.all_to_all(copies, "tensor", 0, 0)

    oth, turned = call(
        other_kernel,
        [((features, width), jnp.float32), ((features, rows), g.dtype)],
        [VMEM, VMEM],
        "weight_grads_other",
        scratch=[pltpu.VMEM((features, rows), g.dtype)],
        flops=work,
        moved=3_000_000,
    )(grads, x)
    got = lax.ppermute(oth, "c", swap)
    (mine,) = call(
        own_kernel, [((features, width), jnp.float32)], [VMEM, VMEM], "weight_grads_own", flops=work, moved=3_000_000
    )(turned, x)

    peers = nz * nx
    (code,) = call(pack_kernel, [((peers, 8, 2 * width + lanes), jnp.int16)], [VMEM] * 3, "pack", moved=4_000_000)(
        mine.reshape(peers, 8, width), got.reshape(peers, 8, width), w
    )
    code = lax.all_to_all(code, ("z", "x"), 0, 0)
    (own_w,) = call(weights_kernel, [((peers, 8, width), w.dtype)], [VMEM], "unpack_weights", moved=1_500_000)(code)
    own_w = own_w.reshape(features, width)
    oth_w = lax.ppermute(own_w, "c", swap)
    scale = 1.0 / math.sqrt(rows * peers * 2)
    (grad_weight,) = call(
        functools.partial(sum_kernel, scale), [((8, width), jnp.float32)], [VMEM], "unpack_sum", moved=1_000_000
    )(code)
    (grad_input,) = call(
        input_kernel,
        [((rows, width), jnp.bfloat16)],
        [VMEM] * 3,
        "input_grads",
        scratch=[pltpu.VMEM((2 * features, width), w.dtype)],
        flops=2 * work,
        moved=4_000_000,
    )(grads, own_w, oth_w)
    return (grad_input, grad_weight)


def solution(mesh):
    dp, ny = mesh.shape["dp"], mesh.shape["tensor"]
    nz, nx = ny, dp // (2 * ny)
    fine = Mesh(mesh.devices.reshape(nz, nx, 2, ny), ("z", "x", "c", "tensor"))
    both = P(("z", "x", "c"), "tensor")
    return jax.shard_map(
        functools.partial(per_device, nz, nx, ny),
        mesh=fine,
        in_specs=(both, both, both, P()),
        out_specs=(both, both),
        check_vma=False,
    )
```

time: 397 us -> 115 us (0.29)
  waiting for transfers between devices: 365 us -> 2.93 us
  blocking collectives: 0 us -> 86 us
  starting transfers between devices: 0.11 us -> 17.1 us
  between operations: 17 us -> 0.7 us
  Pallas kernels: 0 us -> 5.93 us
  other arithmetic: 4.71 us -> 0 us
    unnamed x4 -> x0, waiting for transfers between devices: 219 us -> none
    all_gather x2 -> x0, waiting for transfers between devices: 146 us -> none  [the longest x1 96 us: per_device(): weights = lax.all_gather(w_key, 'dp', axis=0, tiled=True)]
    all_to_all x0 -> x2, blocking collectives: none -> 86 us  [the longest x1 58.5 us: per_device(): code = lax.all_to_all(code, ('z', 'x'), 0, 0)]
    ppermute x0 -> x2, starting transfers between devices: none -> 17.1 us  [the longest x1 12.2 us: per_device(): got = lax.ppermute(oth, 'c', swap)]
    pallas_call x0 -> x7, Pallas kernels: none -> 5.93 us  [the longest x1 1.87 us: per_device(): call(input_kernel, [((rows, width), jnp.bfloat16)], [VMEM] * 3, 'input_gr...]
  transfers between devices with their start and end apart: 3 -> 2, of which waited for: 3 -> 2; matrix products, arithmetic and copies ran while one was open for 1% -> 0% of each run, Pallas kernels for 0% -> 1%
where the time goes in v2:
time: 115 us; the launch traced here: 114 us
  blocking collectives  86 us (75%)
  starting transfers between devices  17.1 us (15%)
  Pallas kernels  5.93 us (5%)
  waiting for transfers between devices  2.93 us (3%)
  local copies, waits for them, and re-layouts  1.56 us (1%)
    all_to_all x1, blocking collectives, per_device(): code = lax.all_to_all(code, ('z', 'x'), 0, 0)  58.5 us
    all_to_all x1, blocking collectives, per_device(): grads = lax.all_to_all(copies, 'tensor', 0, 0)  27.5 us
    ppermute x1, starting transfers between devices, per_device(): got = lax.ppermute(oth, 'c', swap)  12.2 us
    ppermute x1, starting transfers between devices, per_device(): oth_w = lax.ppermute(own_w, 'c', swap)  4.95 us
  transfers between devices with their start and end apart: 2, of which 2 were waited for; matrix products, arithmetic and copies ran while one was open for 0% of the time, Pallas kernels for 1%

profile of v2, /device:TPU:1, one launch (start us, length us, event | category | flops | bytes accessed | tf_op | source)
XLA Modules:
  0.0 114.2 jit_solution(1430356479956243336)
XLA Ops:
  0.6 0.0 copy-start.1
  0.6 0.9 copy-done.1
  1.5 0.0 copy-start.3
  1.5 0.7 copy-done.3
  2.2 0.8 sort.1
  3.0 0.0 copy-start
  3.0 27.5 %all_to_all.10.g_ref = bf16[8,512,128]{2,1,0:T(8,128)(2,1)S(1)} all-to-all(bf16[8,512,128]{2,1,0:T(8,128)(2,1)S(1)} %sort.1), channel_id=1, replica_groups=mesh['z'=8,'x'=8,'c'=2,'tensor'=8] {'tensor'}, dimensions={0} | all-to-all | bytes 2097152 | tf_op jit(solution)/shard_map/all_to_all | solution.py:131
  30.5 0.0 copy-done
  30.5 0.7 weight_grads_other.1
  31.2 0.0 copy-start.2
  31.2 12.2 %collective-permute-start = (f32[512,640]{1,0:T(8,128)S(1)}, f32[512,640]{1,0:T(8,128)S(1)}, u32[]{:S(2)}, u32[]{:S(2)}) collective-permute-start(f32[512,640]{1,0:T(8,128)S(1)} %get-tuple-element.5), channel_id=1, source_target_pairs={{0,8},{8,0},{1,9},{9,1},{2,10},{10,2},{3,11},{11,3},{4,12},{12,4},... | collective-permute-start | bytes 3932168 | tf_op jit(solution)/shard_map/ppermute | solution.py:142
  43.4 0.6 weight_grads_own.1
  44.0 2.1 %collective-permute-done = f32[512,640]{1,0:T(8,128)S(1)} collective-permute-done((f32[512,640]{1,0:T(8,128)S(1)}, f32[512,640]{1,0:T(8,128)S(1)}, u32[]{:S(2)}, u32[]{:S(2)}) %collective-permute-start) | collective-permute-done | bytes 1310752 | tf_op jit(solution)/shard_map/ppermute | solution.py:142
  46.0 0.0 copy-done.2
  46.0 0.4 pack.1
  46.4 58.5 %all_to_all.11.in_ref = s16[64,8,1408]{2,1,0:T(8,128)(2,1)S(1)} all-to-all(s16[64,8,1408]{2,1,0:T(8,128)(2,1)S(1)} %pack.1), channel_id=1, replica_groups=mesh['z'=8,'x'=8,'c'=2,'tensor'=8] {'z','x'}, dimensions={0} | all-to-all | bytes 2883584 | tf_op jit(solution)/shard_map/all_to_all | solution.py:151
  104.9 0.7 unpack_weights.1
  105.7 4.9 %collective-permute-start.1 = (bf16[512,640]{1,0:T(8,128)(2,1)S(1)}, bf16[512,640]{1,0:T(8,128)(2,1)S(1)}, u32[]{:S(2)}, u32[]{:S(2)}) collective-permute-start(bf16[512,640]{1,0:T(8,128)(2,1)S(1)} %bitcast.5), channel_id=1, source_target_pairs={{0,8},{8,0},{1,9},{9,1},{2,10},{10,2},{3,11},{11,3},{4,12},{12,4},... | collective-permute-start | bytes 1966088 | tf_op jit(solution)/shard_map/ppermute | solution.py:154
  110.7 0.8 unpack_sum.1
  111.5 0.9 collective-permute-done.1.oth_ref
  112.4 1.9 %input_grads.1 = bf16[512,640]{1,0:T(8,128)(2,1)} custom-call(bf16[8,512,128]{2,1,0:T(8,128)(2,1)S(1)} %all_to_all.10.g_ref, bf16[512,640]{1,0:T(8,128)(2,1)S(1)} %bitcast.6, bf16[512,640]{1,0:T(8,128)(2,1)S(1)} %collective-permute-done.1.oth_ref), custom_call_target="tpu_custom_call" | custom-call | flops 671088640 | bytes 4000000 | tf_op jit(solution)/shard_map/input_grads/pallas_call | solution.py:159
Async XLA Ops:
  0.6 0.9 copy-start.1
  1.5 0.7 copy-start.3
  3.0 27.5 %copy-start = (bf16[512,640]{1,0:T(8,128)(2,1)S(1)}, bf16[512,640]{1,0:T(8,128)(2,1)}, u32[]{:S(2)}) copy-start(bf16[512,640]{1,0:T(8,128)(2,1)} %x_ref.3) | copy-start | bytes 1966084
  31.2 14.8 %copy-start.2 = (bf16[8,640]{1,0:T(8,128)(2,1)S(1)}, bf16[8,640]{1,0:T(8,128)(2,1)}, u32[]{:S(2)}) copy-start(bf16[8,640]{1,0:T(8,128)(2,1)} %w_ref.1) | copy-start | bytes 30724
  31.2 14.8 %collective-permute-start = (f32[512,640]{1,0:T(8,128)S(1)}, f32[512,640]{1,0:T(8,128)S(1)}, u32[]{:S(2)}, u32[]{:S(2)}) collective-permute-start(f32[512,640]{1,0:T(8,128)S(1)} %get-tuple-element.5), channel_id=1, source_target_pairs={{0,8},{8,0},{1,9},{9,1},{2,10},{10,2},{3,11},{11,3},{4,12},{12,4},... | collective-permute-start | bytes 3932168 | tf_op jit(solution)/shard_map/ppermute | solution.py:142
  105.7 6.7 %collective-permute-start.1 = (bf16[512,640]{1,0:T(8,128)(2,1)S(1)}, bf16[512,640]{1,0:T(8,128)(2,1)S(1)}, u32[]{:S(2)}, u32[]{:S(2)}) collective-permute-start(bf16[512,640]{1,0:T(8,128)(2,1)S(1)} %bitcast.5), channel_id=1, source_target_pairs={{0,8},{8,0},{1,9},{9,1},{2,10},{10,2},{3,11},{11,3},{4,12},{12,4},... | collective-permute-start | bytes 1966088 | tf_op jit(solution)/shard_map/ppermute | solution.py:154

commit v3 on v2

--- a/solution.py
+++ b/solution.py
@@ -10,7 +10,6 @@
 
 STEPS = 256.0
 LARGEST = 32767.0
-BIAS = 127.0
 VMEM = pl.BlockSpec(memory_space=pltpu.VMEM)
 SMEM = pl.BlockSpec(memory_space=pltpu.SMEM)
 
@@ -46,42 +45,21 @@
     out_ref[...] = jnp.dot(g_ref[...], x_ref[...], preferred_element_type=jnp.float32)
 
 
-def pack_kernel(a_ref, b_ref, w_ref, out_ref):
-    rows, width = w_ref.shape
-    lanes = out_ref.shape[2] - 2 * width
-
-    def store(k, at, v):
-        out_ref[k, :, at : at + v.shape[1]] = v.astype(jnp.int32).astype(out_ref.dtype)
-
-    w = w_ref[...].astype(jnp.float32)
-    size = jnp.abs(w)
-    e = jnp.floor(jnp.log2(jnp.maximum(size, 2.0**-126)))
-    bits = (e + BIAS) * 128.0 + (size * jnp.exp2(-e) * 128.0 - 128.0)
-    bits = jnp.where(size < 2.0**-126, 0.0, bits)
-    bits = jnp.round(jnp.where(w < 0.0, -bits, bits))
+def pack_kernel(a_ref, b_ref, out_ref):
+    _, rows, width = a_ref.shape
+    lanes = out_ref.shape[2] - width
     for k in range(out_ref.shape[0]):
         v = a_ref[k] + b_ref[k]
         top = jnp.maximum(jnp.max(jnp.abs(v), axis=1, keepdims=True), 1e-30)
         e = jnp.ceil(STEPS * jnp.log2(top * (1.0 / LARGEST))) + 1.0
-        store(k, 0, jnp.round(v * jnp.exp2(e * (-1.0 / STEPS))))
-        store(k, width, jnp.broadcast_to(e, (rows, lanes)))
-        store(k, width + lanes, bits)
-
-
-def weights_kernel(in_ref, out_ref):
-    width = out_ref.shape[2]
-    for s in range(in_ref.shape[0]):
-        bits = in_ref[s, :, in_ref.shape[2] - width :].astype(jnp.int32)
-        size = jnp.abs(bits)
-        e = (size >> 7).astype(jnp.float32) - BIAS
-        v = ((size & 127) + 128).astype(jnp.float32) * jnp.exp2(e) * (1.0 / 128.0)
-        v = jnp.where(size < 128, 0.0, jnp.where(bits < 0, -v, v))
-        out_ref[s] = v.astype(out_ref.dtype)
+        q = jnp.round(v * jnp.exp2(e * (-1.0 / STEPS)))
+        out_ref[k, :, :width] = q.astype(jnp.int32).astype(out_ref.dtype)
+        out_ref[k, :, width:] = jnp.broadcast_to(e, (rows, lanes)).astype(jnp.int32).astype(out_ref.dtype)
 
 
 def sum_kernel(scale, in_ref, out_ref):
     rows, width = out_ref.shape
-    lanes = in_ref.shape[2] - 2 * width
+    lanes = in_ref.shape[2] - width
     total = [jnp.zeros((rows, lanes), jnp.float32) for _ in range(width // lanes)]
     for s in range(in_ref.shape[0]):
         step = jnp.exp2(in_ref[s, :, width : width + lanes].astype(jnp.int32).astype(jnp.float32) * (1.0 / STEPS))
@@ -129,6 +107,8 @@
         lengths, group.astype(jnp.int32).reshape(1), g
     )
     grads = lax.all_to_all(copies, "tensor", 0, 0)
+    line = lax.all_gather(w, "x", axis=0, tiled=True)
+    grads, line = lax.optimization_barrier((grads, line))
 
     oth, turned = call(
         other_kernel,
@@ -145,12 +125,11 @@
     )(turned, x)
 
     peers = nz * nx
-    (code,) = call(pack_kernel, [((peers, 8, 2 * width + lanes), jnp.int16)], [VMEM] * 3, "pack", moved=4_000_000)(
-        mine.reshape(peers, 8, width), got.reshape(peers, 8, width), w
+    (code,) = call(pack_kernel, [((peers, 8, width + lanes), jnp.int16)], [VMEM] * 2, "pack", moved=4_000_000)(
+        mine.reshape(peers, 8, width), got.reshape(peers, 8, width)
     )
     code = lax.all_to_all(code, ("z", "x"), 0, 0)
-    (own_w,) = call(weights_kernel, [((peers, 8, width), w.dtype)], [VMEM], "unpack_weights", moved=1_500_000)(code)
-    own_w = own_w.reshape(features, width)
+    own_w = lax.all_gather(line, "z", axis=0, tiled=True)
     oth_w = lax.ppermute(own_w, "c", swap)
     scale = 1.0 / math.sqrt(rows * peers * 2)
     (grad_weight,) = call(

time: 115 us -> 118 us (1.026); the launches traced: 114 us -> 116 us
  blocking collectives: 86 us -> 54 us
  starting transfers between devices: 17.1 us -> 49 us
    all_to_all x2 -> x0, blocking collectives: 86 us -> none  [the longest x1 58.5 us: per_device(): code = lax.all_to_all(code, ('z', 'x'), 0, 0)]
    all_gather x0 -> x2, blocking collectives: none -> 54 us  [the longest x1 33.6 us: per_device(): own_w = lax.all_gather(line, 'z', axis=0, tiled=True)]
    all_to_all x0 -> x2, starting transfers between devices: none -> 26 us  [the longest x1 17.8 us: per_device(): code = lax.all_to_all(code, ('z', 'x'), 0, 0)]
    ppermute x1, starting transfers between devices: 12.2 us -> 15.7 us  [per_device(): got = lax.ppermute(oth, 'c', swap)]
    ppermute x1, starting transfers between devices: 4.95 us -> 7.23 us  [per_device(): oth_w = lax.ppermute(own_w, 'c', swap)]
  transfers between devices with their start and end apart: 2 -> 4, of which waited for: 2 -> 2; matrix products, arithmetic and copies ran while one was open for 0% -> 0% of each run, Pallas kernels for 1% -> 2%
where the time goes in v3:
time: 118 us; the launch traced here: 116 us
  blocking collectives  54 us (46%)
  starting transfers between devices  49 us (42%)
  Pallas kernels  6.97 us (6%)
  waiting for transfers between devices  3.77 us (3%)
  local copies, waits for them, and re-layouts  1.56 us (1%)
    all_gather x1, blocking collectives, per_device(): own_w = lax.all_gather(line, 'z', axis=0, tiled=True)  33.6 us
    all_gather x1, blocking collectives, per_device(): line = lax.all_gather(w, 'x', axis=0, tiled=True)  20.4 us
    all_to_all x1, starting transfers between devices, per_device(): code = lax.all_to_all(code, ('z', 'x'), 0, 0)  17.8 us
    ppermute x1, starting transfers between devices, per_device(): got = lax.ppermute(oth, 'c', swap)  15.7 us
    all_to_all x1, starting transfers between devices, per_device(): grads = lax.all_to_all(copies, 'tensor', 0, 0)  8.24 us
    ppermute x1, starting transfers between devices, per_device(): oth_w = lax.ppermute(own_w, 'c', swap)  7.23 us
  transfers between devices with their start and end apart: 4, of which 2 were waited for; matrix products, arithmetic and copies ran while one was open for 0% of the time, Pallas kernels for 2%

profile of v3, /device:TPU:1, one launch (start us, length us, event | category | flops | bytes accessed | tf_op | source)
XLA Modules:
  0.0 116.0 jit_solution(15657698553714632832)
XLA Ops:
  0.6 0.0 copy-start.1
  0.6 0.9 copy-done.1
  1.5 0.0 copy-start.2
  1.5 0.7 copy-done.2
  2.2 1.8 %sort.1 = bf16[8,512,128]{2,1,0:T(8,128)(2,1)} custom-call(s32[128]{0:T(128)S(1)} %copy-done.2, s32[1]{0:T(128)} %bitcast.place_ref, bf16[512,128]{1,0:T(8,128)(2,1)S(1)} %copy-done.1), custom_call_target="tpu_custom_call" | custom-call | bytes 2000000 | tf_op jit(solution)/shard_map/sort/pallas_call | solution.py:106
  4.0 0.0 copy-start.3
  4.0 0.0 copy-start
  4.0 8.2 %all-to-all-start = ((bf16[8,512,128]{2,1,0:T(8,128)(2,1)}), bf16[8,512,128]{2,1,0:T(8,128)(2,1)S(1)}, u32[]{:S(2)}, u32[]{:S(2)}) async-start(bf16[8,512,128]{2,1,0:T(8,128)(2,1)} %sort.1), calls=%async_computation | async-start | bytes 2097152 | tf_op jit(solution)/shard_map/all_to_all | solution.py:109
  12.2 0.0 copy-done.3
  12.2 20.4 %all_gather.6 = bf16[64,640]{1,0:T(8,128)(2,1)S(1)} all-gather(bf16[8,640]{1,0:T(8,128)(2,1)S(1)} %copy-done.3), channel_id=1, replica_groups=mesh['z'=8,'x'=8,'c'=2,'tensor'=8] {'x'}, dimensions={0}, use_global_device_ids=true | all-gather | bytes 92160 | tf_op jit(solution)/shard_map/all_gather | solution.py:110
  32.6 0.0 all-to-all-done.g_ref
  32.6 0.0 copy-done
  32.6 0.7 weight_grads_other.1
  33.3 15.7 %collective-permute-start.1 = (f32[512,640]{1,0:T(8,128)S(1)}, f32[512,640]{1,0:T(8,128)S(1)}, u32[]{:S(2)}, u32[]{:S(2)}) collective-permute-start(f32[512,640]{1,0:T(8,128)S(1)} %get-tuple-element.9), channel_id=1, source_target_pairs={{0,8},{8,0},{1,9},{9,1},{2,10},{10,2},{3,11},{11,3},{4,12},{12,4},... | collective-permute-start | bytes 3932168 | tf_op jit(solution)/shard_map/ppermute | solution.py:122
  49.1 0.6 weight_grads_own.1
  49.6 2.1 %collective-permute-done.1 = f32[512,640]{1,0:T(8,128)S(1)} collective-permute-done((f32[512,640]{1,0:T(8,128)S(1)}, f32[512,640]{1,0:T(8,128)S(1)}, u32[]{:S(2)}, u32[]{:S(2)}) %collective-permute-start.1) | collective-permute-done | bytes 1310752 | tf_op jit(solution)/shard_map/ppermute | solution.py:122
  51.7 1.2 %pack.1 = s16[64,8,768]{2,1,0:T(8,128)(2,1)} custom-call(f32[64,8,640]{2,1,0:T(8,128)S(1)} %bitcast.3, f32[64,8,640]{2,1,0:T(8,128)S(1)} %bitcast.4), custom_call_target="tpu_custom_call" | custom-call | bytes 4000000 | tf_op jit(solution)/shard_map/pack/pallas_call | solution.py:128
  52.9 17.8 %all-to-all-start.1 = ((s16[64,8,768]{2,1,0:T(8,128)(2,1)}), s16[64,8,768]{2,1,0:T(8,128)(2,1)S(1)}, u32[]{:S(2)}, u32[]{:S(2)}) async-start(s16[64,8,768]{2,1,0:T(8,128)(2,1)} %pack.1), calls=%async_computation.1 | async-start | bytes 1572864 | tf_op jit(solution)/shard_map/all_to_all | solution.py:131
  70.7 33.6 %all_gather.7.own_ref = bf16[512,640]{1,0:T(8,128)(2,1)S(1)} all-gather(bf16[64,640]{1,0:T(8,128)(2,1)S(1)} %all_gather.6), channel_id=1, replica_groups=mesh['z'=8,'x'=8,'c'=2,'tensor'=8] {'z'}, dimensions={0}, use_global_device_ids=true | all-gather | bytes 737280 | tf_op jit(solution)/shard_map/all_gather | solution.py:132
  104.4 7.2 %collective-permute-start = (bf16[512,640]{1,0:T(8,128)(2,1)S(1)}, bf16[512,640]{1,0:T(8,128)(2,1)S(1)}, u32[]{:S(2)}, u32[]{:S(2)}) collective-permute-start(bf16[512,640]{1,0:T(8,128)(2,1)S(1)} %all_gather.7.own_ref), channel_id=1, source_target_pairs={{0,8},{8,0},{1,9},{9,1},{2,10},{10,2},{3,11},{11,3},{4,12},{12,4},... | collective-permute-start | bytes 1966088 | tf_op jit(solution)/shard_map/ppermute | solution.py:133
  111.6 1.7 %collective-permute-done.oth_ref = bf16[512,640]{1,0:T(8,128)(2,1)S(1)} collective-permute-done((bf16[512,640]{1,0:T(8,128)(2,1)S(1)}, bf16[512,640]{1,0:T(8,128)(2,1)S(1)}, u32[]{:S(2)}, u32[]{:S(2)}) %collective-permute-start) | collective-permute-done | bytes 655392 | tf_op jit(solution)/shard_map/ppermute | solution.py:133
  113.3 1.9 %input_grads.1 = bf16[512,640]{1,0:T(8,128)(2,1)} custom-call(bf16[8,512,128]{2,1,0:T(8,128)(2,1)S(1)} %all-to-all-done.g_ref, bf16[512,640]{1,0:T(8,128)(2,1)S(1)} %all_gather.7.own_ref, bf16[512,640]{1,0:T(8,128)(2,1)S(1)} %collective-permute-done.oth_ref), custom_call_target="tpu_custom_call" | custom-call | flops 671088640 | bytes 4000000 | tf_op jit(solution)/shard_map/input_grads/pallas_call | solution.py:138
  115.1 0.0 all-to-all-done.1.in_ref
  115.2 0.8 unpack_sum.1
Async XLA Ops:
  0.6 0.9 copy-start.1
  1.5 0.7 copy-start.2
  4.0 8.2 %copy-start.3 = (bf16[8,640]{1,0:T(8,128)(2,1)S(1)}, bf16[8,640]{1,0:T(8,128)(2,1)}, u32[]{:S(2)}) copy-start(bf16[8,640]{1,0:T(8,128)(2,1)} %param.6) | copy-start | bytes 30724
  4.0 28.6 %copy-start = (bf16[512,640]{1,0:T(8,128)(2,1)S(1)}, bf16[512,640]{1,0:T(8,128)(2,1)}, u32[]{:S(2)}) copy-start(bf16[512,640]{1,0:T(8,128)(2,1)} %x_ref.3) | copy-start | bytes 1966084
  4.0 28.6 %all-to-all-start = ((bf16[8,512,128]{2,1,0:T(8,128)(2,1)}), bf16[8,512,128]{2,1,0:T(8,128)(2,1)S(1)}, u32[]{:S(2)}, u32[]{:S(2)}) async-start(bf16[8,512,128]{2,1,0:T(8,128)(2,1)} %sort.1), calls=%async_computation | async-start | bytes 2097152 | tf_op jit(solution)/shard_map/all_to_all | solution.py:109
  33.3 18.4 %collective-permute-start.1 = (f32[512,640]{1,0:T(8,128)S(1)}, f32[512,640]{1,0:T(8,128)S(1)}, u32[]{:S(2)}, u32[]{:S(2)}) collective-permute-start(f32[512,640]{1,0:T(8,128)S(1)} %get-tuple-element.9), channel_id=1, source_target_pairs={{0,8},{8,0},{1,9},{9,1},{2,10},{10,2},{3,11},{11,3},{4,12},{12,4},... | collective-permute-start | bytes 3932168 | tf_op jit(solution)/shard_map/ppermute | solution.py:122
  52.9 62.2 %all-to-all-start.1 = ((s16[64,8,768]{2,1,0:T(8,128)(2,1)}), s16[64,8,768]{2,1,0:T(8,128)(2,1)S(1)}, u32[]{:S(2)}, u32[]{:S(2)}) async-start(s16[64,8,768]{2,1,0:T(8,128)(2,1)} %pack.1), calls=%async_computation.1 | async-start | bytes 1572864 | tf_op jit(solution)/shard_map/all_to_all | solution.py:131
  104.4 8.9 %collective-permute-start = (bf16[512,640]{1,0:T(8,128)(2,1)S(1)}, bf16[512,640]{1,0:T(8,128)(2,1)S(1)}, u32[]{:S(2)}, u32[]{:S(2)}) collective-permute-start(bf16[512,640]{1,0:T(8,128)(2,1)S(1)} %all_gather.7.own_ref), channel_id=1, source_target_pairs={{0,8},{8,0},{1,9},{9,1},{2,10},{10,2},{3,11},{11,3},{4,12},{12,4},... | collective-permute-start | bytes 1966088 | tf_op jit(solution)/shard_map/ppermute | solution.py:133

commit v4 on v3

--- a/solution.py
+++ b/solution.py
@@ -107,8 +107,8 @@
         lengths, group.astype(jnp.int32).reshape(1), g
     )
     grads = lax.all_to_all(copies, "tensor", 0, 0)
-    line = lax.all_gather(w, "x", axis=0, tiled=True)
-    grads, line = lax.optimization_barrier((grads, line))
+    own_w = lax.all_gather(w, ("z", "x"), axis=0, tiled=True)
+    grads, own_w = lax.optimization_barrier((grads, own_w))
 
     oth, turned = call(
         other_kernel,
@@ -128,8 +128,8 @@
     (code,) = call(pack_kernel, [((peers, 8, width + lanes), jnp.int16)], [VMEM] * 2, "pack", moved=4_000_000)(
         mine.reshape(peers, 8, width), got.reshape(peers, 8, width)
     )
+    code, own_w = lax.optimization_barrier((code, own_w))
     code = lax.all_to_all(code, ("z", "x"), 0, 0)
-    own_w = lax.all_gather(line, "z", axis=0, tiled=True)
     oth_w = lax.ppermute(own_w, "c", swap)
     scale = 1.0 / math.sqrt(rows * peers * 2)
     (grad_weight,) = call(

time: 118 us -> 115 us (0.975)
  starting transfers between devices: 49 us -> 30.8 us
  waiting for transfers between devices: 3.77 us -> 20.2 us
    all_to_all x1, waiting for transfers between devices: 0.01 us -> 16.4 us  [per_device(): code = lax.all_to_all(code, ('z', 'x'), 0, 0)]
    all_to_all x1, starting transfers between devices: 17.8 us -> 7.38 us  [per_device(): code = lax.all_to_all(code, ('z', 'x'), 0, 0)]
    ppermute x1, starting transfers between devices: 7.23 us -> 2.56 us  [per_device(): oth_w = lax.ppermute(own_w, 'c', swap)]
    ppermute x1, starting transfers between devices: 15.7 us -> 12.6 us  [per_device(): got = lax.ppermute(oth, 'c', swap)]
    all_gather x2 -> x1, blocking collectives: 54 us -> 53.5 us  [per_device(): own_w = lax.all_gather(w, ('z', 'x'), axis=0, tiled=True)]
  transfers between devices with their start and end apart: 4 -> 4, of which waited for: 2 -> 3; matrix products, arithmetic and copies ran while one was open for 0% -> 0% of each run, Pallas kernels for 2% -> 2%
where the time goes in v4:
time: 115 us; the launch traced here: 114 us
  blocking collectives  53.5 us (47%)
  starting transfers between devices  30.8 us (27%)
  waiting for transfers between devices  20.2 us (18%)
  Pallas kernels  6.96 us (6%)
  local copies, waits for them, and re-layouts  1.56 us (1%)
    all_gather x1, blocking collectives, per_device(): own_w = lax.all_gather(w, ('z', 'x'), axis=0, tiled=True)  53.5 us
    all_to_all x1, waiting for transfers between devices, per_device(): code = lax.all_to_all(code, ('z', 'x'), 0, 0)  16.4 us
    ppermute x1, starting transfers between devices, per_device(): got = lax.ppermute(oth, 'c', swap)  12.6 us
    all_to_all x1, starting transfers between devices, per_device(): grads = lax.all_to_all(copies, 'tensor', 0, 0)  8.24 us
    all_to_all x1, starting transfers between devices, per_device(): code = lax.all_to_all(code, ('z', 'x'), 0, 0)  7.38 us
    ppermute x1, starting transfers between devices, per_device(): oth_w = lax.ppermute(own_w, 'c', swap)  2.56 us
  transfers between devices with their start and end apart: 4, of which 3 were waited for; matrix products, arithmetic and copies ran while one was open for 0% of the time, Pallas kernels for 2%

profile of v4, /device:TPU:1, one launch (start us, length us, event | category | flops | bytes accessed | tf_op | source)
XLA Modules:
  0.0 113.7 jit_solution(4630195526027066643)
XLA Ops:
  0.6 0.0 copy-start.1
  0.6 0.9 copy-done.1
  1.5 0.0 copy-start.2
  1.5 0.7 copy-done.2
  2.2 1.8 %sort.1 = bf16[8,512,128]{2,1,0:T(8,128)(2,1)} custom-call(s32[128]{0:T(128)S(1)} %copy-done.2, s32[1]{0:T(128)} %bitcast.place_ref, bf16[512,128]{1,0:T(8,128)(2,1)S(1)} %copy-done.1), custom_call_target="tpu_custom_call" | custom-call | bytes 2000000 | tf_op jit(solution)/shard_map/sort/pallas_call | solution.py:106
  4.0 0.0 copy-start.3
  4.0 0.0 copy-start
  4.0 8.2 %all-to-all-start = ((bf16[8,512,128]{2,1,0:T(8,128)(2,1)}), bf16[8,512,128]{2,1,0:T(8,128)(2,1)S(1)}, u32[]{:S(2)}, u32[]{:S(2)}) async-start(bf16[8,512,128]{2,1,0:T(8,128)(2,1)} %sort.1), calls=%async_computation | async-start | bytes 2097152 | tf_op jit(solution)/shard_map/all_to_all | solution.py:109
  12.2 0.0 copy-done.3
  12.2 53.5 %all_gather.3.own_ref = bf16[512,640]{1,0:T(8,128)(2,1)S(1)} all-gather(bf16[8,640]{1,0:T(8,128)(2,1)S(1)} %copy-done.3), channel_id=1, replica_groups=mesh['z'=8,'x'=8,'c'=2,'tensor'=8] {'z','x'}, dimensions={0}, use_global_device_ids=true | all-gather | bytes 665600 | tf_op jit(solution)/shard_map/all_gather | solution.py:110
  65.7 0.0 all-to-all-done.g_ref
  65.7 0.0 copy-done
  65.7 0.7 weight_grads_other.1
  66.5 12.6 %collective-permute-start = (f32[512,640]{1,0:T(8,128)S(1)}, f32[512,640]{1,0:T(8,128)S(1)}, u32[]{:S(2)}, u32[]{:S(2)}) collective-permute-start(f32[512,640]{1,0:T(8,128)S(1)} %get-tuple-element.10), channel_id=1, source_target_pairs={{0,8},{8,0},{1,9},{9,1},{2,10},{10,2},{3,11},{11,3},{4,12},{12,4},... | collective-permute-start | bytes 3932168 | tf_op jit(solution)/shard_map/ppermute | solution.py:122
  79.1 0.6 weight_grads_own.1
  79.6 2.1 %collective-permute-done = f32[512,640]{1,0:T(8,128)S(1)} collective-permute-done((f32[512,640]{1,0:T(8,128)S(1)}, f32[512,640]{1,0:T(8,128)S(1)}, u32[]{:S(2)}, u32[]{:S(2)}) %collective-permute-start) | collective-permute-done | bytes 1310752 | tf_op jit(solution)/shard_map/ppermute | solution.py:122
  81.7 1.2 %pack.1 = s16[64,8,768]{2,1,0:T(8,128)(2,1)} custom-call(f32[64,8,640]{2,1,0:T(8,128)S(1)} %bitcast.3, f32[64,8,640]{2,1,0:T(8,128)S(1)} %bitcast.4), custom_call_target="tpu_custom_call" | custom-call | bytes 4000000 | tf_op jit(solution)/shard_map/pack/pallas_call | solution.py:128
  82.9 7.4 %all-to-all-start.1 = ((s16[64,8,768]{2,1,0:T(8,128)(2,1)}), s16[64,8,768]{2,1,0:T(8,128)(2,1)S(1)}, u32[]{:S(2)}, u32[]{:S(2)}) async-start(s16[64,8,768]{2,1,0:T(8,128)(2,1)} %pack.1), calls=%async_computation.1 | async-start | bytes 1572864 | tf_op jit(solution)/shard_map/all_to_all | solution.py:132
  90.3 2.6 %collective-permute-start.1 = (bf16[512,640]{1,0:T(8,128)(2,1)S(1)}, bf16[512,640]{1,0:T(8,128)(2,1)S(1)}, u32[]{:S(2)}, u32[]{:S(2)}) collective-permute-start(bf16[512,640]{1,0:T(8,128)(2,1)S(1)} %all_gather.3.own_ref), channel_id=1, source_target_pairs={{0,8},{8,0},{1,9},{9,1},{2,10},{10,2},{3,11},{11,3},{4,12},{12,4},... | collective-permute-start | bytes 1966088 | tf_op jit(solution)/shard_map/ppermute | solution.py:133
  92.9 1.7 %collective-permute-done.1.oth_ref = bf16[512,640]{1,0:T(8,128)(2,1)S(1)} collective-permute-done((bf16[512,640]{1,0:T(8,128)(2,1)S(1)}, bf16[512,640]{1,0:T(8,128)(2,1)S(1)}, u32[]{:S(2)}, u32[]{:S(2)}) %collective-permute-start.1) | collective-permute-done | bytes 655392 | tf_op jit(solution)/shard_map/ppermute | solution.py:133
  94.6 1.9 %input_grads.1 = bf16[512,640]{1,0:T(8,128)(2,1)} custom-call(bf16[8,512,128]{2,1,0:T(8,128)(2,1)S(1)} %all-to-all-done.g_ref, bf16[512,640]{1,0:T(8,128)(2,1)S(1)} %all_gather.3.own_ref, bf16[512,640]{1,0:T(8,128)(2,1)S(1)} %collective-permute-done.1.oth_ref), custom_call_target="tpu_custom_call" | custom-call | flops 671088640 | bytes 4000000 | tf_op jit(solution)/shard_map/input_grads/pallas_call | solution.py:138
  96.4 16.4 %all-to-all-done.1.in_ref = s16[64,8,768]{2,1,0:T(8,128)(2,1)S(1)} async-done(((s16[64,8,768]{2,1,0:T(8,128)(2,1)}), s16[64,8,768]{2,1,0:T(8,128)(2,1)S(1)}, u32[]{:S(2)}, u32[]{:S(2)}) %all-to-all-start.1) | async-done | bytes 786464 | tf_op jit(solution)/shard_map/all_to_all | solution.py:132
  112.9 0.8 unpack_sum.1
Async XLA Ops:
  0.6 0.9 copy-start.1
  1.5 0.7 copy-start.2
  4.0 8.2 %copy-start.3 = (bf16[8,640]{1,0:T(8,128)(2,1)S(1)}, bf16[8,640]{1,0:T(8,128)(2,1)}, u32[]{:S(2)}) copy-start(bf16[8,640]{1,0:T(8,128)(2,1)} %param.6) | copy-start | bytes 30724
  4.0 61.8 %copy-start = (bf16[512,640]{1,0:T(8,128)(2,1)S(1)}, bf16[512,640]{1,0:T(8,128)(2,1)}, u32[]{:S(2)}) copy-start(bf16[512,640]{1,0:T(8,128)(2,1)} %x_ref.3) | copy-start | bytes 1966084
  4.0 61.7 %all-to-all-start = ((bf16[8,512,128]{2,1,0:T(8,128)(2,1)}), bf16[8,512,128]{2,1,0:T(8,128)(2,1)S(1)}, u32[]{:S(2)}, u32[]{:S(2)}) async-start(bf16[8,512,128]{2,1,0:T(8,128)(2,1)} %sort.1), calls=%async_computation | async-start | bytes 2097152 | tf_op jit(solution)/shard_map/all_to_all | solution.py:109
  66.5 15.2 %collective-permute-start = (f32[512,640]{1,0:T(8,128)S(1)}, f32[512,640]{1,0:T(8,128)S(1)}, u32[]{:S(2)}, u32[]{:S(2)}) collective-permute-start(f32[512,640]{1,0:T(8,128)S(1)} %get-tuple-element.10), channel_id=1, source_target_pairs={{0,8},{8,0},{1,9},{9,1},{2,10},{10,2},{3,11},{11,3},{4,12},{12,4},... | collective-permute-start | bytes 3932168 | tf_op jit(solution)/shard_map/ppermute | solution.py:122
  82.9 30.0 %all-to-all-start.1 = ((s16[64,8,768]{2,1,0:T(8,128)(2,1)}), s16[64,8,768]{2,1,0:T(8,128)(2,1)S(1)}, u32[]{:S(2)}, u32[]{:S(2)}) async-start(s16[64,8,768]{2,1,0:T(8,128)(2,1)} %pack.1), calls=%async_computation.1 | async-start | bytes 1572864 | tf_op jit(solution)/shard_map/all_to_all | solution.py:132
  90.3 4.3 %collective-permute-start.1 = (bf16[512,640]{1,0:T(8,128)(2,1)S(1)}, bf16[512,640]{1,0:T(8,128)(2,1)S(1)}, u32[]{:S(2)}, u32[]{:S(2)}) collective-permute-start(bf16[512,640]{1,0:T(8,128)(2,1)S(1)} %all_gather.3.own_ref), channel_id=1, source_target_pairs={{0,8},{8,0},{1,9},{9,1},{2,10},{10,2},{3,11},{11,3},{4,12},{12,4},... | collective-permute-start | bytes 1966088 | tf_op jit(solution)/shard_map/ppermute | solution.py:133

commit v5 on v4

--- a/solution.py
+++ b/solution.py
@@ -14,8 +14,8 @@
 SMEM = pl.BlockSpec(memory_space=pltpu.SMEM)
 
 
-def sort_kernel(lengths_ref, place_ref, g_ref, out_ref):
-    rows, width = g_ref.shape
+def other_kernel(lengths_ref, place_ref, g_ref, x_ref, oth_ref, own_ref, sorted_ref, turned_ref):
+    blocks, rows, width = g_ref.shape
     half = width // 2
     core = place_ref[0] % 2
     length = lengths_ref[place_ref[0]]
@@ -24,18 +24,12 @@
     inner = place % half
     kind = jnp.where(place < half, core, 1 - core)
     order = jnp.where(take == (inner // 8) * 16 + inner % 8 + 8 * kind, 1.0, 0.0).astype(g_ref.dtype)
-    g = jnp.dot(g_ref[...], order, preferred_element_type=jnp.float32)
     live = lax.broadcasted_iota(jnp.int32, (rows, width), 0) < length
-    g = jnp.where(live, g, 0.0).astype(out_ref.dtype)
-    for k in range(out_ref.shape[0]):
-        out_ref[k] = g
-
-
-def other_kernel(g_ref, x_ref, oth_ref, own_ref, turned_ref):
-    blocks, rows, width = g_ref.shape
-    half = width // 2
     for k in range(blocks):
-        turned = g_ref[k].T
+        g = jnp.dot(g_ref[k], order, preferred_element_type=jnp.float32)
+        g = jnp.where(live, g, 0.0).astype(g_ref.dtype)
+        sorted_ref[k] = g
+        turned = g.T
         own_ref[k * half : (k + 1) * half, :] = turned[:half]
         turned_ref[k * half : (k + 1) * half, :] = turned[half:]
     oth_ref[...] = jnp.dot(turned_ref[...], x_ref[...], preferred_element_type=jnp.float32)
@@ -103,22 +97,19 @@
     group = (lax.axis_index("z") * nx + lax.axis_index("x")) * 2 + lax.axis_index("c")
     swap = [(0, 1), (1, 0)]
 
-    (copies,) = call(sort_kernel, [((ny, rows, block), g.dtype)], [SMEM, SMEM, VMEM], "sort", moved=2_000_000)(
-        lengths, group.astype(jnp.int32).reshape(1), g
-    )
-    grads = lax.all_to_all(copies, "tensor", 0, 0)
-    own_w = lax.all_gather(w, ("z", "x"), axis=0, tiled=True)
+    grads = lax.all_gather(g, "tensor", axis=0, tiled=True)
+    own_w = lax.all_to_all(jnp.broadcast_to(w[None], (nz * nx,) + w.shape), ("z", "x"), 0, 0).reshape(features, width)
     grads, own_w = lax.optimization_barrier((grads, own_w))
 
-    oth, turned = call(
+    oth, turned, grads = call(
         other_kernel,
-        [((features, width), jnp.float32), ((features, rows), g.dtype)],
-        [VMEM, VMEM],
+        [((features, width), jnp.float32), ((features, rows), g.dtype), ((ny, rows, block), g.dtype)],
+        [SMEM, SMEM, VMEM, VMEM],
         "weight_grads_other",
         scratch=[pltpu.VMEM((features, rows), g.dtype)],
         flops=work,
         moved=3_000_000,
-    )(grads, x)
+    )(lengths, group.astype(jnp.int32).reshape(1), grads.reshape(ny, rows, block), x)
     got = lax.ppermute(oth, "c", swap)
     (mine,) = call(
         own_kernel, [((features, width), jnp.float32)], [VMEM, VMEM], "weight_grads_own", flops=work, moved=3_000_000

time: 115 us -> 121 us (1.052)
  blocking collectives: 53.5 us -> 0 us
  waiting for transfers between devices: 20.2 us -> 50.6 us
  starting transfers between devices: 30.8 us -> 46.1 us
  between operations: 0.7 us -> 14.1 us
  local copies, waits for them, and re-layouts: 1.56 us -> 2.82 us
    all_gather x1 -> x0, blocking collectives: 53.5 us -> none  [per_device(): own_w = lax.all_gather(w, ('z', 'x'), axis=0, tiled=True)]
    all_to_all x1, waiting for transfers between devices: 0.01 us -> 19.1 us  [per_device(): lax.all_to_all(jnp.broadcast_to(w[None], (nz * nx,) + w.shape), ('z', 'x'...]
    all_to_all x1, starting transfers between devices: 8.24 us -> 23.2 us  [per_device(): lax.all_to_all(jnp.broadcast_to(w[None], (nz * nx,) + w.shape), ('z', 'x'...]
    all_gather x0 -> x1, waiting for transfers between devices: none -> 10.6 us  [per_device(): grads = lax.all_gather(g, 'tensor', axis=0, tiled=True)]
    all_to_all x1, starting transfers between devices: 7.38 us -> 13.5 us  [per_device(): code = lax.all_to_all(code, ('z', 'x'), 0, 0)]
    ppermute x1, starting transfers between devices: 12.6 us -> 6.87 us  [per_device(): got = lax.ppermute(oth, 'c', swap)]
    pallas_call x1 -> x0, Pallas kernels: 1.76 us -> none  [per_device(): call(sort_kernel, [((ny, rows, block), g.dtype)], [SMEM, SMEM, VMEM], 'so...]
    broadcast_in_dim x0 -> x1, local copies, waits for them, and re-layouts: none -> 1.59 us  [per_device(): jnp.broadcast_to(w[None], (nz * nx,) + w.shape)]
  transfers between devices with their start and end apart: 4 -> 5, of which waited for: 3 -> 5; matrix products, arithmetic and copies ran while one was open for 0% -> 1% of each run, Pallas kernels for 2% -> 2%
where the time goes in v5:
time: 121 us; the launch traced here: 120 us
  waiting for transfers between devices  50.6 us (42%)
  starting transfers between devices  46.1 us (38%)
  between operations  14.1 us (12%)
  Pallas kernels  5.92 us (5%)
  local copies, waits for them, and re-layouts  2.82 us (2%)
    all_to_all x1, starting transfers between devices, per_device(): lax.all_to_all(jnp.broadcast_to(w[None], (nz * nx,) + w.shape), ('z', 'x'...  23.2 us
    all_to_all x1, waiting for transfers between devices, per_device(): lax.all_to_all(jnp.broadcast_to(w[None], (nz * nx,) + w.shape), ('z', 'x'...  19.1 us
    all_to_all x1, waiting for transfers between devices, per_device(): code = lax.all_to_all(code, ('z', 'x'), 0, 0)  16.4 us
    all_to_all x1, starting transfers between devices, per_device(): code = lax.all_to_all(code, ('z', 'x'), 0, 0)  13.5 us
    all_gather x1, waiting for transfers between devices, per_device(): grads = lax.all_gather(g, 'tensor', axis=0, tiled=True)  10.6 us
    ppermute x1, starting transfers between devices, per_device(): got = lax.ppermute(oth, 'c', swap)  6.87 us
    ppermute x1, starting transfers between devices, per_device(): oth_w = lax.ppermute(own_w, 'c', swap)  2.56 us
  transfers between devices with their start and end apart: 5, of which 5 were waited for; matrix products, arithmetic and copies ran while one was open for 1% of the time, Pallas kernels for 2%

profile of v5, /device:TPU:1, one launch (start us, length us, event | category | flops | bytes accessed | tf_op | source)
XLA Modules:
  0.0 119.6 jit_solution(17765316631773502847)
XLA Ops:
  7.2 0.0 copy-start
  7.2 0.0 copy-start.2
  7.2 0.0 all-gather.2.cloned.1.call-start
  7.2 0.7 all-gather.2.cloned.1.call-update
  7.9 1.6 %broadcast_in_dim.2 = bf16[64,8,640]{2,1,0:T(8,128)(2,1)} broadcast(bf16[8,640]{1,0:T(8,128)(2,1)} %param.6), dimensions={1,2} | broadcast | bytes 665600 | tf_op jit(solution)/shard_map/broadcast_in_dim | solution.py:101
  9.5 23.2 %all-to-all-start = ((bf16[64,8,640]{2,1,0:T(8,128)(2,1)}), bf16[64,8,640]{2,1,0:T(8,128)(2,1)S(1)}, u32[]{:S(2)}, u32[]{:S(2)}) async-start(bf16[64,8,640]{2,1,0:T(8,128)(2,1)} %broadcast_in_dim.2), calls=%async_computation | async-start | bytes 1310720 | tf_op jit(solution)/shard_map/all_to_all | solution.py:101
  32.7 19.1 %all-to-all-done = bf16[64,8,640]{2,1,0:T(8,128)(2,1)S(1)} async-done(((bf16[64,8,640]{2,1,0:T(8,128)(2,1)}), bf16[64,8,640]{2,1,0:T(8,128)(2,1)S(1)}, u32[]{:S(2)}, u32[]{:S(2)}) %all-to-all-start) | async-done | bytes 655392 | tf_op jit(solution)/shard_map/all_to_all | solution.py:101
  51.8 10.6 %all-gather.2.cloned.1.call-done = bf16[4096,128]{1,0:T(8,128)(2,1)} async-done(((bf16[512,128]{1,0:T(8,128)(2,1)}), bf16[4096,128]{1,0:T(8,128)(2,1)}) %all-gather.2.cloned.1.call-update) | async-done | bytes 1048592 | tf_op jit(solution)/shard_map/all_gather | solution.py:100
  62.4 0.0 copy-done
  62.4 0.0 copy-done.2
  62.4 0.0 copy-start.1
  62.4 1.2 %copy-done.1 = bf16[4096,128]{1,0:T(8,128)(2,1)S(1)} copy-done((bf16[4096,128]{1,0:T(8,128)(2,1)S(1)}, bf16[4096,128]{1,0:T(8,128)(2,1)}, u32[]{:S(2)}) %copy-start.1) | copy-done | bytes 1048600
  63.6 1.4 %weight_grads_other.1 = (f32[512,640]{1,0:T(8,128)S(1)}, bf16[512,512]{1,0:T(8,128)(2,1)S(1)}, bf16[8,512,128]{2,1,0:T(8,128)(2,1)S(1)}) custom-call(s32[128]{0:T(128)S(1)} %copy-done.2, s32[1]{0:T(128)} %bitcast.place_ref, bf16[8,512,128]{2,1,0:T(8,128)(2,1)S(1)} %bitcast.9, bf16[512,640]{1,0:T(8,128)(2,1)S(1)} %copy-done), custom_call_target="tpu_custom_call" | custom-call | flops 335544320 | bytes 3000000 | tf_op jit(solution)/shard_map/weight_grads_other/pallas_call | solution.py:104
  65.1 6.9 %collective-permute-start = (f32[512,640]{1,0:T(8,128)S(1)}, f32[512,640]{1,0:T(8,128)S(1)}, u32[]{:S(2)}, u32[]{:S(2)}) collective-permute-start(f32[512,640]{1,0:T(8,128)S(1)} %get-tuple-element.12), channel_id=1, source_target_pairs={{0,8},{8,0},{1,9},{9,1},{2,10},{10,2},{3,11},{11,3},{4,12},{12,4},... | collective-permute-start | bytes 3932168 | tf_op jit(solution)/shard_map/ppermute | solution.py:113
  72.0 0.6 weight_grads_own.1
  72.5 2.1 %collective-permute-done = f32[512,640]{1,0:T(8,128)S(1)} collective-permute-done((f32[512,640]{1,0:T(8,128)S(1)}, f32[512,640]{1,0:T(8,128)S(1)}, u32[]{:S(2)}, u32[]{:S(2)}) %collective-permute-start) | collective-permute-done | bytes 1310752 | tf_op jit(solution)/shard_map/ppermute | solution.py:113
  74.6 1.2 %pack.1 = s16[64,8,768]{2,1,0:T(8,128)(2,1)} custom-call(f32[64,8,640]{2,1,0:T(8,128)S(1)} %bitcast.5, f32[64,8,640]{2,1,0:T(8,128)S(1)} %bitcast.8), custom_call_target="tpu_custom_call" | custom-call | bytes 4000000 | tf_op jit(solution)/shard_map/pack/pallas_call | solution.py:119
  75.8 13.5 %all-to-all-start.1 = ((s16[64,8,768]{2,1,0:T(8,128)(2,1)}), s16[64,8,768]{2,1,0:T(8,128)(2,1)S(1)}, u32[]{:S(2)}, u32[]{:S(2)}) async-start(s16[64,8,768]{2,1,0:T(8,128)(2,1)} %pack.1), calls=%async_computation.1 | async-start | bytes 1572864 | tf_op jit(solution)/shard_map/all_to_all | solution.py:123
  89.3 2.6 %collective-permute-start.1 = (bf16[512,640]{1,0:T(8,128)(2,1)S(1)}, bf16[512,640]{1,0:T(8,128)(2,1)S(1)}, u32[]{:S(2)}, u32[]{:S(2)}) collective-permute-start(bf16[512,640]{1,0:T(8,128)(2,1)S(1)} %bitcast.6), channel_id=1, source_target_pairs={{0,8},{8,0},{1,9},{9,1},{2,10},{10,2},{3,11},{11,3},{4,12},{12,4},... | collective-permute-start | bytes 1966088 | tf_op jit(solution)/shard_map/ppermute | solution.py:124
  91.9 1.7 %collective-permute-done.1.oth_ref = bf16[512,640]{1,0:T(8,128)(2,1)S(1)} collective-permute-done((bf16[512,640]{1,0:T(8,128)(2,1)S(1)}, bf16[512,640]{1,0:T(8,128)(2,1)S(1)}, u32[]{:S(2)}, u32[]{:S(2)}) %collective-permute-start.1) | collective-permute-done | bytes 655392 | tf_op jit(solution)/shard_map/ppermute | solution.py:124
  93.6 1.9 %input_grads.1 = bf16[512,640]{1,0:T(8,128)(2,1)} custom-call(bf16[8,512,128]{2,1,0:T(8,128)(2,1)S(1)} %get-tuple-element.10.g_ref, bf16[512,640]{1,0:T(8,128)(2,1)S(1)} %bitcast.7, bf16[512,640]{1,0:T(8,128)(2,1)S(1)} %collective-permute-done.1.oth_ref), custom_call_target="tpu_custom_call" | custom-call | flops 671088640 | bytes 4000000 | tf_op jit(solution)/shard_map/input_grads/pallas_call | solution.py:129
  95.4 16.4 %all-to-all-done.1.in_ref = s16[64,8,768]{2,1,0:T(8,128)(2,1)S(1)} async-done(((s16[64,8,768]{2,1,0:T(8,128)(2,1)}), s16[64,8,768]{2,1,0:T(8,128)(2,1)S(1)}, u32[]{:S(2)}, u32[]{:S(2)}) %all-to-all-start.1) | async-done | bytes 786464 | tf_op jit(solution)/shard_map/all_to_all | solution.py:123
  111.9 0.8 unpack_sum.1
Async XLA Ops:
  7.2 55.2 %copy-start = (bf16[512,640]{1,0:T(8,128)(2,1)S(1)}, bf16[512,640]{1,0:T(8,128)(2,1)}, u32[]{:S(2)}) copy-start(bf16[512,640]{1,0:T(8,128)(2,1)} %x_ref.3) | copy-start | bytes 1966084
  7.2 55.2 %copy-start.2 = (s32[128]{0:T(128)S(1)}, s32[128]{0:T(128)}, u32[]{:S(2)}) copy-start(s32[128]{0:T(128)} %lengths_ref.1) | copy-start | bytes 1540
  7.2 55.2 %all-gather.2.cloned.1.call-start = ((), (), s32[]{:S(2)}) async-start(), calls=%async_computation.2 | async-start | bytes 1179648 | tf_op jit(solution)/shard_map/all_gather | solution.py:100
  9.5 42.3 %all-to-all-start = ((bf16[64,8,640]{2,1,0:T(8,128)(2,1)}), bf16[64,8,640]{2,1,0:T(8,128)(2,1)S(1)}, u32[]{:S(2)}, u32[]{:S(2)}) async-start(bf16[64,8,640]{2,1,0:T(8,128)(2,1)} %broadcast_in_dim.2), calls=%async_computation | async-start | bytes 1310720 | tf_op jit(solution)/shard_map/all_to_all | solution.py:101
  62.4 1.2 %copy-start.1 = (bf16[4096,128]{1,0:T(8,128)(2,1)S(1)}, bf16[4096,128]{1,0:T(8,128)(2,1)}, u32[]{:S(2)}) copy-start(bf16[4096,128]{1,0:T(8,128)(2,1)} %all-gather.2.cloned.1.call-done) | copy-start | bytes 3145732
  65.1 9.5 %collective-permute-start = (f32[512,640]{1,0:T(8,128)S(1)}, f32[512,640]{1,0:T(8,128)S(1)}, u32[]{:S(2)}, u32[]{:S(2)}) collective-permute-start(f32[512,640]{1,0:T(8,128)S(1)} %get-tuple-element.12), channel_id=1, source_target_pairs={{0,8},{8,0},{1,9},{9,1},{2,10},{10,2},{3,11},{11,3},{4,12},{12,4},... | collective-permute-start | bytes 3932168 | tf_op jit(solution)/shard_map/ppermute | solution.py:113
  75.8 36.1 %all-to-all-start.1 = ((s16[64,8,768]{2,1,0:T(8,128)(2,1)}), s16[64,8,768]{2,1,0:T(8,128)(2,1)S(1)}, u32[]{:S(2)}, u32[]{:S(2)}) async-start(s16[64,8,768]{2,1,0:T(8,128)(2,1)} %pack.1), calls=%async_computation.1 | async-start | bytes 1572864 | tf_op jit(solution)/shard_map/all_to_all | solution.py:123
  89.3 4.3 %collective-permute-start.1 = (bf16[512,640]{1,0:T(8,128)(2,1)S(1)}, bf16[512,640]{1,0:T(8,128)(2,1)S(1)}, u32[]{:S(2)}, u32[]{:S(2)}) collective-permute-start(bf16[512,640]{1,0:T(8,128)(2,1)S(1)} %bitcast.6), channel_id=1, source_target_pairs={{0,8},{8,0},{1,9},{9,1},{2,10},{10,2},{3,11},{11,3},{4,12},{12,4},... | collective-permute-start | bytes 1966088 | tf_op jit(solution)/shard_map/ppermute | solution.py:124
Sparse Core Ops, SparseCore 0:
  10.7 51.6 all-gather.1

commit v6 on v5

--- a/solution.py
+++ b/solution.py
@@ -14,10 +14,13 @@
 SMEM = pl.BlockSpec(memory_space=pltpu.SMEM)
 
 
-def other_kernel(lengths_ref, place_ref, g_ref, x_ref, oth_ref, own_ref, sorted_ref, turned_ref):
-    blocks, rows, width = g_ref.shape
+def other_kernel(lengths_ref, place_ref, g_ref, rest_ref, x_ref, oth_ref, own_ref, sorted_ref, turned_ref):
+    blocks, _, width = g_ref.shape
+    rows = x_ref.shape[0]
+    bits = blocks.bit_length() - 1
     half = width // 2
     core = place_ref[0] % 2
+    me = place_ref[1]
     length = lengths_ref[place_ref[0]]
     take = lax.broadcasted_iota(jnp.int32, (width, width), 0)
     place = lax.broadcasted_iota(jnp.int32, (width, width), 1)
@@ -26,7 +29,11 @@
     order = jnp.where(take == (inner // 8) * 16 + inner % 8 + 8 * kind, 1.0, 0.0).astype(g_ref.dtype)
     live = lax.broadcasted_iota(jnp.int32, (rows, width), 0) < length
     for k in range(blocks):
-        g = jnp.dot(g_ref[k], order, preferred_element_type=jnp.float32)
+        at = 0
+        for b in range(bits):
+            at = at + (((k >> b) % 2 + me // 2**b) % 2) * 2 ** (bits - 1 - b)
+        parts = [g_ref[k], rest_ref[at]]
+        g = jnp.concatenate([jnp.dot(p, order, preferred_element_type=jnp.float32) for p in parts], axis=0)
         g = jnp.where(live, g, 0.0).astype(g_ref.dtype)
         sorted_ref[k] = g
         turned = g.T
@@ -97,19 +104,25 @@
     group = (lax.axis_index("z") * nx + lax.axis_index("x")) * 2 + lax.axis_index("c")
     swap = [(0, 1), (1, 0)]
 
-    grads = lax.all_gather(g, "tensor", axis=0, tiled=True)
+    rest = min(16, rows // 2)
+    ends = g[None, rows - rest :]
+    far = ny // 2
+    while far:
+        ends = jnp.concatenate([ends, lax.ppermute(ends, "tensor", [(i, i ^ far) for i in range(ny)])], axis=0)
+        far //= 2
+    grads = lax.all_gather(g[: rows - rest], "tensor", axis=0, tiled=False)
     own_w = lax.all_to_all(jnp.broadcast_to(w[None], (nz * nx,) + w.shape), ("z", "x"), 0, 0).reshape(features, width)
-    grads, own_w = lax.optimization_barrier((grads, own_w))
+    grads, ends, own_w = lax.optimization_barrier((grads, ends, own_w))
 
     oth, turned, grads = call(
         other_kernel,
         [((features, width), jnp.float32), ((features, rows), g.dtype), ((ny, rows, block), g.dtype)],
-        [SMEM, SMEM, VMEM, VMEM],
+        [SMEM, SMEM, VMEM, VMEM, VMEM],
         "weight_grads_other",
         scratch=[pltpu.VMEM((features, rows), g.dtype)],
         flops=work,
         moved=3_000_000,
-    )(lengths, group.astype(jnp.int32).reshape(1), grads.reshape(ny, rows, block), x)
+    )(lengths, jnp.stack([group, lax.axis_index("tensor")]).astype(jnp.int32), grads, ends, x)
     got = lax.ppermute(oth, "c", swap)
     (mine,) = call(
         own_kernel, [((features, width), jnp.float32)], [VMEM, VMEM], "weight_grads_own", flops=work, moved=3_000_000

time: 121 us -> 120 us (level)
  waiting for transfers between devices: 50.6 us -> 23.2 us
  blocking collectives: 0 us -> 23.2 us
  starting transfers between devices: 46.1 us -> 62.9 us
  between operations: 14.1 us -> 0.76 us
    all_gather x0 -> x1, blocking collectives: none -> 23.2 us  [per_device(): grads = lax.all_gather(g[:rows - rest], 'tensor', axis=0, tiled=False)]
    all_to_all x1, waiting for transfers between devices: 19.1 us -> 0.01 us  [per_device(): lax.all_to_all(jnp.broadcast_to(w[None], (nz * nx,) + w.shape), ('z', 'x'...]
    ppermute x0 -> x3, starting transfers between devices: none -> 14.4 us  [per_device(): lax.ppermute(ends, 'tensor', [(i, i ^ far) for i in range(ny)])]
    all_gather x1 -> x0, waiting for transfers between devices: 10.6 us -> none  [per_device(): grads = lax.all_gather(g, 'tensor', axis=0, tiled=True)]
    ppermute x1, starting transfers between devices: 6.87 us -> 10.3 us  [per_device(): got = lax.ppermute(oth, 'c', swap)]
    ppermute x0 -> x3, waiting for transfers between devices: none -> 3.01 us  [per_device(): lax.ppermute(ends, 'tensor', [(i, i ^ far) for i in range(ny)])]
    unnamed x6, local copies, waits for them, and re-layouts: 1.23 us -> 0.01 us
  transfers between devices with their start and end apart: 5 -> 7, of which waited for: 5 -> 5; matrix products, arithmetic and copies ran while one was open for 1% -> 0% of each run, Pallas kernels for 2% -> 2%
where the time goes in v6:
time: 120 us; the launch traced here: 118 us
  starting transfers between devices  62.9 us (52%)
  waiting for transfers between devices  23.2 us (19%)
  blocking collectives  23.2 us (19%)
  Pallas kernels  6.25 us (5%)
  local copies, waits for them, and re-layouts  1.65 us (1%)
    all_to_all x1, starting transfers between devices, per_device(): lax.all_to_all(jnp.broadcast_to(w[None], (nz * nx,) + w.shape), ('z', 'x'...  23.3 us
    all_gather x1, blocking collectives, per_device(): grads = lax.all_gather(g[:rows - rest], 'tensor', axis=0, tiled=False)  23.2 us
    all_to_all x1, waiting for transfers between devices, per_device(): code = lax.all_to_all(code, ('z', 'x'), 0, 0)  16.4 us
    ppermute x3, starting transfers between devices, per_device(): lax.ppermute(ends, 'tensor', [(i, i ^ far) for i in range(ny)])  14.4 us
    all_to_all x1, starting transfers between devices, per_device(): code = lax.all_to_all(code, ('z', 'x'), 0, 0)  12.4 us
    ppermute x1, starting transfers between devices, per_device(): got = lax.ppermute(oth, 'c', swap)  10.3 us
    ppermute x3, waiting for transfers between devices, per_device(): lax.ppermute(ends, 'tensor', [(i, i ^ far) for i in range(ny)])  3.01 us
    ppermute x1, starting transfers between devices, per_device(): oth_w = lax.ppermute(own_w, 'c', swap)  2.56 us
  transfers between devices with their start and end apart: 7, of which 5 were waited for; matrix products, arithmetic and copies ran while one was open for 0% of the time, Pallas kernels for 2%

profile of v6, /device:TPU:1, one launch (start us, length us, event | category | flops | bytes accessed | tf_op | source)
XLA Modules:
  0.0 118.0 jit_solution(5254793137421353270)
XLA Ops:
  0.6 0.0 copy-start.2
  0.6 0.0 slice-start
  0.7 1.6 %broadcast_in_dim.10 = bf16[64,8,640]{2,1,0:T(8,128)(2,1)} broadcast(bf16[8,640]{1,0:T(8,128)(2,1)} %param.6), dimensions={1,2} | broadcast | bytes 665600 | tf_op jit(solution)/shard_map/broadcast_in_dim | solution.py:114
  2.3 0.0 copy-start
  2.3 0.0 copy-start.1
  2.3 23.3 %all-to-all-start = ((bf16[64,8,640]{2,1,0:T(8,128)(2,1)}), bf16[64,8,640]{2,1,0:T(8,128)(2,1)S(1)}, u32[]{:S(2)}, u32[]{:S(2)}) async-start(bf16[64,8,640]{2,1,0:T(8,128)(2,1)} %broadcast_in_dim.10), calls=%async_computation | async-start | bytes 1310720 | tf_op jit(solution)/shard_map/all_to_all | solution.py:114
  25.6 0.0 copy-done.2
  25.6 7.9 %collective-permute-start = (bf16[1,16,128]{2,1,0:T(8,128)(2,1)S(1)}, bf16[1,16,128]{2,1,0:T(8,128)(2,1)S(1)}, u32[]{:S(2)}, u32[]{:S(2)}) collective-permute-start(bf16[1,16,128]{2,1,0:T(8,128)(2,1)S(1)} %slice_bitcast_fusion), channel_id=1, source_target_pairs={{0,4},{1,5},{2,6},{3,7},{4,0},{5,1},{6,2},{7,3},{8,12},{9,13},{10,... | collective-permute-start | bytes 12296 | tf_op jit(solution)/shard_map/ppermute | solution.py:111
  33.5 1.3 %collective-permute-done = bf16[1,16,128]{2,1,0:T(8,128)(2,1)S(1)} collective-permute-done((bf16[1,16,128]{2,1,0:T(8,128)(2,1)S(1)}, bf16[1,16,128]{2,1,0:T(8,128)(2,1)S(1)}, u32[]{:S(2)}, u32[]{:S(2)}) %collective-permute-start) | collective-permute-done | bytes 4128 | tf_op jit(solution)/shard_map/ppermute | solution.py:111
  34.8 3.8 %collective-permute-start.1 = (bf16[2,16,128]{2,1,0:T(8,128)(2,1)S(1)}, bf16[2,16,128]{2,1,0:T(8,128)(2,1)S(1)}, u32[]{:S(2)}, u32[]{:S(2)}) collective-permute-start(bf16[2,16,128]{2,1,0:T(8,128)(2,1)S(1)} %pad_maximum_fusion.2), channel_id=1, source_target_pairs={{0,2},{1,3},{2,0},{3,1},{4,6},{5,7},{6,4},{7,5},{8,10},{9,11},{10,... | collective-permute-start | bytes 24584 | tf_op jit(solution)/shard_map/ppermute | solution.py:111
  38.6 0.0 slice-done
  38.6 23.2 %all-gather = bf16[3968,128]{1,0:T(8,128)(2,1)S(1)} all-gather(bf16[496,128]{1,0:T(8,128)(2,1)S(1)} %slice-done), channel_id=2, replica_groups=mesh['z'=8,'x'=8,'c'=2,'tensor'=8] {'tensor'}, dimensions={0}, use_global_device_ids=true | all-gather | bytes 1142784 | tf_op jit(solution)/shard_map/all_gather | solution.py:113
  61.8 0.0 collective-permute-done.1
  61.8 2.7 %collective-permute-start.2 = (bf16[4,16,128]{2,1,0:T(8,128)(2,1)S(1)}, bf16[4,16,128]{2,1,0:T(8,128)(2,1)S(1)}, u32[]{:S(2)}, u32[]{:S(2)}) collective-permute-start(bf16[4,16,128]{2,1,0:T(8,128)(2,1)S(1)} %pad_maximum_fusion.1), channel_id=1, source_target_pairs={{0,1},{1,0},{2,3},{3,2},{4,5},{5,4},{6,7},{7,6},{8,9},{9,8},{10,11... | collective-permute-start | bytes 49160 | tf_op jit(solution)/shard_map/ppermute | solution.py:111
  64.5 0.1 pad_add_fusion.place_ref
  64.6 1.7 %collective-permute-done.2 = bf16[4,16,128]{2,1,0:T(8,128)(2,1)S(1)} collective-permute-done((bf16[4,16,128]{2,1,0:T(8,128)(2,1)S(1)}, bf16[4,16,128]{2,1,0:T(8,128)(2,1)S(1)}, u32[]{:S(2)}, u32[]{:S(2)}) %collective-permute-start.2) | collective-permute-done | bytes 16416 | tf_op jit(solution)/shard_map/ppermute | solution.py:111
  66.3 0.0 all-to-all-done
  66.3 0.0 copy-done
  66.3 0.0 copy-done.1
  66.3 1.7 %weight_grads_other.1 = (f32[512,640]{1,0:T(8,128)S(1)}, bf16[512,512]{1,0:T(8,128)(2,1)S(1)}, bf16[8,512,128]{2,1,0:T(8,128)(2,1)S(1)}) custom-call(s32[128]{0:T(128)S(1)} %copy-done.1, s32[2]{0:T(128)S(1)} %pad_add_fusion.place_ref, bf16[8,496,128]{2,1,0:T(8,128)(2,1)S(1)} %bitcast.9, bf16[8,16,128]{2,1,0:T(8,128)(2,1)S(1)} %pad_maximum_fusion.rest_ref, ...), custom_call_target="tpu_custom_call" | custom-call | flops 335544320 | bytes 3000000 | tf_op jit(solution)/shard_map/weight_grads_other/pallas_call | solution.py:117
  68.1 10.3 %collective-permute-start.3 = (f32[512,640]{1,0:T(8,128)S(1)}, f32[512,640]{1,0:T(8,128)S(1)}, u32[]{:S(2)}, u32[]{:S(2)}) collective-permute-start(f32[512,640]{1,0:T(8,128)S(1)} %get-tuple-element.14), channel_id=1, source_target_pairs={{0,8},{8,0},{1,9},{9,1},{2,10},{10,2},{3,11},{11,3},{4,12},{12,4},... | collective-permute-start | bytes 3932168 | tf_op jit(solution)/shard_map/ppermute | solution.py:126
  78.3 0.6 weight_grads_own.1
  78.9 2.1 %collective-permute-done.3 = f32[512,640]{1,0:T(8,128)S(1)} collective-permute-done((f32[512,640]{1,0:T(8,128)S(1)}, f32[512,640]{1,0:T(8,128)S(1)}, u32[]{:S(2)}, u32[]{:S(2)}) %collective-permute-start.3) | collective-permute-done | bytes 1310752 | tf_op jit(solution)/shard_map/ppermute | solution.py:126
  81.0 1.2 %pack.1 = s16[64,8,768]{2,1,0:T(8,128)(2,1)} custom-call(f32[64,8,640]{2,1,0:T(8,128)S(1)} %bitcast.8, f32[64,8,640]{2,1,0:T(8,128)S(1)} %bitcast.12), custom_call_target="tpu_custom_call" | custom-call | bytes 4000000 | tf_op jit(solution)/shard_map/pack/pallas_call | solution.py:132
  82.2 12.4 %all-to-all-start.1 = ((s16[64,8,768]{2,1,0:T(8,128)(2,1)}), s16[64,8,768]{2,1,0:T(8,128)(2,1)S(1)}, u32[]{:S(2)}, u32[]{:S(2)}) async-start(s16[64,8,768]{2,1,0:T(8,128)(2,1)} %pack.1), calls=%async_computation.1 | async-start | bytes 1572864 | tf_op jit(solution)/shard_map/all_to_all | solution.py:136
  94.6 2.6 %collective-permute-start.4 = (bf16[512,640]{1,0:T(8,128)(2,1)S(1)}, bf16[512,640]{1,0:T(8,128)(2,1)S(1)}, u32[]{:S(2)}, u32[]{:S(2)}) collective-permute-start(bf16[512,640]{1,0:T(8,128)(2,1)S(1)} %bitcast.10), channel_id=1, source_target_pairs={{0,8},{8,0},{1,9},{9,1},{2,10},{10,2},{3,11},{11,3},{4,12},{12,4},... | collective-permute-start | bytes 1966088 | tf_op jit(solution)/shard_map/ppermute | solution.py:137
  97.2 1.7 %collective-permute-done.4.oth_ref = bf16[512,640]{1,0:T(8,128)(2,1)S(1)} collective-permute-done((bf16[512,640]{1,0:T(8,128)(2,1)S(1)}, bf16[512,640]{1,0:T(8,128)(2,1)S(1)}, u32[]{:S(2)}, u32[]{:S(2)}) %collective-permute-start.4) | collective-permute-done | bytes 655392 | tf_op jit(solution)/shard_map/ppermute | solution.py:137
  98.9 1.9 %input_grads.1 = bf16[512,640]{1,0:T(8,128)(2,1)} custom-call(bf16[8,512,128]{2,1,0:T(8,128)(2,1)S(1)} %get-tuple-element.12.g_ref, bf16[512,640]{1,0:T(8,128)(2,1)S(1)} %bitcast.11, bf16[512,640]{1,0:T(8,128)(2,1)S(1)} %collective-permute-done.4.oth_ref), custom_call_target="tpu_custom_call" | custom-call | flops 671088640 | bytes 4000000 | tf_op jit(solution)/shard_map/input_grads/pallas_call | solution.py:142
  100.7 16.4 %all-to-all-done.1.in_ref = s16[64,8,768]{2,1,0:T(8,128)(2,1)S(1)} async-done(((s16[64,8,768]{2,1,0:T(8,128)(2,1)}), s16[64,8,768]{2,1,0:T(8,128)(2,1)S(1)}, u32[]{:S(2)}, u32[]{:S(2)}) %all-to-all-start.1) | async-done | bytes 786464 | tf_op jit(solution)/shard_map/all_to_all | solution.py:136
  117.2 0.8 unpack_sum.1
  (4 shorter events, 0.0 us)
Async XLA Ops:
  0.6 25.0 %copy-start.2 = (bf16[512,128]{1,0:T(8,128)(2,1)S(1)}, bf16[512,128]{1,0:T(8,128)(2,1)}, u32[]{:S(2)}) copy-start(bf16[512,128]{1,0:T(8,128)(2,1)} %param.5) | copy-start | bytes 393220
  0.6 38.0 %slice-start = ((bf16[512,128]{1,0:T(8,128)(2,1)}), bf16[496,128]{1,0:T(8,128)(2,1)S(1)}, s32[]{:S(2)}) async-start(bf16[512,128]{1,0:T(8,128)(2,1)} %param.5), calls=%async_computation.2 | async-start | bytes 253952 | tf_op jit(solution)/shard_map/slice | solution.py:113
  2.3 64.0 %copy-start = (bf16[512,640]{1,0:T(8,128)(2,1)S(1)}, bf16[512,640]{1,0:T(8,128)(2,1)}, u32[]{:S(2)}) copy-start(bf16[512,640]{1,0:T(8,128)(2,1)} %x_ref.3) | copy-start | bytes 1966084
  2.3 64.0 %copy-start.1 = (s32[128]{0:T(128)S(1)}, s32[128]{0:T(128)}, u32[]{:S(2)}) copy-start(s32[128]{0:T(128)} %lengths_ref.1) | copy-start | bytes 1540
  2.3 64.0 %all-to-all-start = ((bf16[64,8,640]{2,1,0:T(8,128)(2,1)}), bf16[64,8,640]{2,1,0:T(8,128)(2,1)S(1)}, u32[]{:S(2)}, u32[]{:S(2)}) async-start(bf16[64,8,640]{2,1,0:T(8,128)(2,1)} %broadcast_in_dim.10), calls=%async_computation | async-start | bytes 1310720 | tf_op jit(solution)/shard_map/all_to_all | solution.py:114
  25.6 9.2 %collective-permute-start = (bf16[1,16,128]{2,1,0:T(8,128)(2,1)S(1)}, bf16[1,16,128]{2,1,0:T(8,128)(2,1)S(1)}, u32[]{:S(2)}, u32[]{:S(2)}) collective-permute-start(bf16[1,16,128]{2,1,0:T(8,128)(2,1)S(1)} %slice_bitcast_fusion), channel_id=1, source_target_pairs={{0,4},{1,5},{2,6},{3,7},{4,0},{5,1},{6,2},{7,3},{8,12},{9,13},{10,... | collective-permute-start | bytes 12296 | tf_op jit(solution)/shard_map/ppermute | solution.py:111
  34.8 27.0 %collective-permute-start.1 = (bf16[2,16,128]{2,1,0:T(8,128)(2,1)S(1)}, bf16[2,16,128]{2,1,0:T(8,128)(2,1)S(1)}, u32[]{:S(2)}, u32[]{:S(2)}) collective-permute-start(bf16[2,16,128]{2,1,0:T(8,128)(2,1)S(1)} %pad_maximum_fusion.2), channel_id=1, source_target_pairs={{0,2},{1,3},{2,0},{3,1},{4,6},{5,7},{6,4},{7,5},{8,10},{9,11},{10,... | collective-permute-start | bytes 24584 | tf_op jit(solution)/shard_map/ppermute | solution.py:111
  61.8 4.5 %collective-permute-start.2 = (bf16[4,16,128]{2,1,0:T(8,128)(2,1)S(1)}, bf16[4,16,128]{2,1,0:T(8,128)(2,1)S(1)}, u32[]{:S(2)}, u32[]{:S(2)}) collective-permute-start(bf16[4,16,128]{2,1,0:T(8,128)(2,1)S(1)} %pad_maximum_fusion.1), channel_id=1, source_target_pairs={{0,1},{1,0},{2,3},{3,2},{4,5},{5,4},{6,7},{7,6},{8,9},{9,8},{10,11... | collective-permute-start | bytes 49160 | tf_op jit(solution)/shard_map/ppermute | solution.py:111
  68.1 12.9 %collective-permute-start.3 = (f32[512,640]{1,0:T(8,128)S(1)}, f32[512,640]{1,0:T(8,128)S(1)}, u32[]{:S(2)}, u32[]{:S(2)}) collective-permute-start(f32[512,640]{1,0:T(8,128)S(1)} %get-tuple-element.14), channel_id=1, source_target_pairs={{0,8},{8,0},{1,9},{9,1},{2,10},{10,2},{3,11},{11,3},{4,12},{12,4},... | collective-permute-start | bytes 3932168 | tf_op jit(solution)/shard_map/ppermute | solution.py:126
  82.2 34.9 %all-to-all-start.1 = ((s16[64,8,768]{2,1,0:T(8,128)(2,1)}), s16[64,8,768]{2,1,0:T(8,128)(2,1)S(1)}, u32[]{:S(2)}, u32[]{:S(2)}) async-start(s16[64,8,768]{2,1,0:T(8,128)(2,1)} %pack.1), calls=%async_computation.1 | async-start | bytes 1572864 | tf_op jit(solution)/shard_map/all_to_all | solution.py:136
  94.6 4.3 %collective-permute-start.4 = (bf16[512,640]{1,0:T(8,128)(2,1)S(1)}, bf16[512,640]{1,0:T(8,128)(2,1)S(1)}, u32[]{:S(2)}, u32[]{:S(2)}) collective-permute-start(bf16[512,640]{1,0:T(8,128)(2,1)S(1)} %bitcast.10), channel_id=1, source_target_pairs={{0,8},{8,0},{1,9},{9,1},{2,10},{10,2},{3,11},{11,3},{4,12},{12,4},... | collective-permute-start | bytes 1966088 | tf_op jit(solution)/shard_map/ppermute | solution.py:137

commit v7 on v2

--- a/solution.py
+++ b/solution.py
@@ -12,21 +12,28 @@
 LARGEST = 32767.0
 BIAS = 127.0
 VMEM = pl.BlockSpec(memory_space=pltpu.VMEM)
+HBM = pl.BlockSpec(memory_space=pltpu.HBM)
 SMEM = pl.BlockSpec(memory_space=pltpu.SMEM)
 
 
-def sort_kernel(lengths_ref, place_ref, g_ref, out_ref):
+def sort_kernel(place_ref, lengths_ref, in_ref, out_ref, known_ref, g_ref, known_sem, g_sem):
+    known = pltpu.make_async_copy(lengths_ref, known_ref, known_sem)
+    grads = pltpu.make_async_copy(in_ref, g_ref, g_sem)
+    known.start()
+    grads.start()
     rows, width = g_ref.shape
     half = width // 2
     core = place_ref[0] % 2
-    length = lengths_ref[place_ref[0]]
     take = lax.broadcasted_iota(jnp.int32, (width, width), 0)
     place = lax.broadcasted_iota(jnp.int32, (width, width), 1)
     inner = place % half
     kind = jnp.where(place < half, core, 1 - core)
     order = jnp.where(take == (inner // 8) * 16 + inner % 8 + 8 * kind, 1.0, 0.0).astype(g_ref.dtype)
+    slot = lax.broadcasted_iota(jnp.int32, (rows, width), 0)
+    known.wait()
+    live = slot < known_ref[place_ref[0]]
+    grads.wait()
     g = jnp.dot(g_ref[...], order, preferred_element_type=jnp.float32)
-    live = lax.broadcasted_iota(jnp.int32, (rows, width), 0) < length
     g = jnp.where(live, g, 0.0).astype(out_ref.dtype)
     for k in range(out_ref.shape[0]):
         out_ref[k] = g
@@ -46,7 +53,11 @@
     out_ref[...] = jnp.dot(g_ref[...], x_ref[...], preferred_element_type=jnp.float32)
 
 
-def pack_kernel(a_ref, b_ref, w_ref, out_ref):
+def turned_place(k, lines, line):
+    return k % line * lines + k // line
+
+
+def pack_kernel(line, a_ref, b_ref, w_ref, out_ref):
     rows, width = w_ref.shape
     lanes = out_ref.shape[2] - 2 * width
 
@@ -59,8 +70,9 @@
     bits = (e + BIAS) * 128.0 + (size * jnp.exp2(-e) * 128.0 - 128.0)
     bits = jnp.where(size < 2.0**-126, 0.0, bits)
     bits = jnp.round(jnp.where(w < 0.0, -bits, bits))
-    for k in range(out_ref.shape[0]):
-        v = a_ref[k] + b_ref[k]
+    for s in range(out_ref.shape[0]):
+        k = turned_place(s, out_ref.shape[0] // line, line)
+        v = a_ref[s] + b_ref[s]
         top = jnp.maximum(jnp.max(jnp.abs(v), axis=1, keepdims=True), 1e-30)
         e = jnp.ceil(STEPS * jnp.log2(top * (1.0 / LARGEST))) + 1.0
         store(k, 0, jnp.round(v * jnp.exp2(e * (-1.0 / STEPS))))
@@ -68,15 +80,16 @@
         store(k, width + lanes, bits)
 
 
-def weights_kernel(in_ref, out_ref):
+def weights_kernel(line, in_ref, out_ref):
     width = out_ref.shape[2]
-    for s in range(in_ref.shape[0]):
+    for k in range(in_ref.shape[0]):
+        s = turned_place(k, in_ref.shape[0] // line, line)
         bits = in_ref[s, :, in_ref.shape[2] - width :].astype(jnp.int32)
         size = jnp.abs(bits)
         e = (size >> 7).astype(jnp.float32) - BIAS
         v = ((size & 127) + 128).astype(jnp.float32) * jnp.exp2(e) * (1.0 / 128.0)
         v = jnp.where(size < 128, 0.0, jnp.where(bits < 0, -v, v))
-        out_ref[s] = v.astype(out_ref.dtype)
+        out_ref[k] = v.astype(out_ref.dtype)
 
 
 def sum_kernel(scale, in_ref, out_ref):
@@ -92,22 +105,31 @@
         out_ref[:, t * lanes : (t + 1) * lanes] = total[t] * scale
 
 
-def input_kernel(g_ref, own_ref, oth_ref, out_ref, w_ref):
+def input_kernel(g_ref, own_ref, oth_ref, out_ref, w_ref, part_ref, sems):
     blocks, rows, width = g_ref.shape
     half = width // 2
     for k in range(blocks):
         w_ref[k * width : k * width + half, :] = own_ref[k * half : (k + 1) * half, :]
         w_ref[k * width + half : (k + 1) * width, :] = oth_ref[k * half : (k + 1) * half, :]
-    g = jnp.concatenate([g_ref[k] for k in range(blocks)], axis=1)
-    out_ref[...] = jnp.dot(g, w_ref[...], preferred_element_type=jnp.float32).astype(out_ref.dtype)
-
-
-def call(kernel, out, specs, name, scratch=(), flops=0, moved=0):
+    parts = sems.shape[0]
+    size = rows // parts
+    copies = []
+    for i in range(parts):
+        at = slice(i * size, (i + 1) * size)
+        g = jnp.concatenate([g_ref[k, at, :] for k in range(blocks)], axis=1)
+        part_ref[at, :] = jnp.dot(g, w_ref[...], preferred_element_type=jnp.float32).astype(out_ref.dtype)
+        copies.append(pltpu.make_async_copy(part_ref.at[at], out_ref.at[at], sems.at[i]))
+        copies[-1].start()
+    for copy in copies:
+        copy.wait()
+
+
+def call(kernel, out, specs, name, scratch=(), flops=0, moved=0, place=VMEM):
     return pl.pallas_call(
         kernel,
         out_shape=[jax.ShapeDtypeStruct(*o) for o in out],
         in_specs=specs,
-        out_specs=[VMEM] * len(out),
+        out_specs=[place] * len(out),
         scratch_shapes=scratch,
         compiler_params=pltpu.CompilerParams(vmem_limit_bytes=14 * 1024 * 1024),
         cost_estimate=pl.CostEstimate(flops=flops, bytes_accessed=moved, transcendentals=0),
@@ -125,9 +147,19 @@
     group = (lax.axis_index("z") * nx + lax.axis_index("x")) * 2 + lax.axis_index("c")
     swap = [(0, 1), (1, 0)]
 
-    (copies,) = call(sort_kernel, [((ny, rows, block), g.dtype)], [SMEM, SMEM, VMEM], "sort", moved=2_000_000)(
-        lengths, group.astype(jnp.int32).reshape(1), g
-    )
+    (copies,) = call(
+        sort_kernel,
+        [((ny, rows, block), g.dtype)],
+        [SMEM, HBM, HBM],
+        "sort",
+        scratch=[
+            pltpu.SMEM(lengths.shape, lengths.dtype),
+            pltpu.VMEM((rows, block), g.dtype),
+            pltpu.SemaphoreType.DMA,
+            pltpu.SemaphoreType.DMA,
+        ],
+        moved=2_000_000,
+    )(group.astype(jnp.int32).reshape(1), lengths, g)
     grads = lax.all_to_all(copies, "tensor", 0, 0)
 
     oth, turned = call(
@@ -145,11 +177,11 @@
     )(turned, x)
 
     peers = nz * nx
-    (code,) = call(pack_kernel, [((peers, 8, 2 * width + lanes), jnp.int16)], [VMEM] * 3, "pack", moved=4_000_000)(
+    (code,) = call(functools.partial(pack_kernel, nx), [((peers, 8, 2 * width + lanes), jnp.int16)], [VMEM] * 3, "pack", moved=4_000_000)(
         mine.reshape(peers, 8, width), got.reshape(peers, 8, width), w
     )
-    code = lax.all_to_all(code, ("z", "x"), 0, 0)
-    (own_w,) = call(weights_kernel, [((peers, 8, width), w.dtype)], [VMEM], "unpack_weights", moved=1_500_000)(code)
+    code = lax.all_to_all(code, ("x", "z"), 0, 0)
+    (own_w,) = call(functools.partial(weights_kernel, nx), [((peers, 8, width), w.dtype)], [VMEM], "unpack_weights", moved=1_500_000)(code)
     own_w = own_w.reshape(features, width)
     oth_w = lax.ppermute(own_w, "c", swap)
     scale = 1.0 / math.sqrt(rows * peers * 2)
@@ -161,9 +193,14 @@
         [((rows, width), jnp.bfloat16)],
         [VMEM] * 3,
         "input_grads",
-        scratch=[pltpu.VMEM((2 * features, width), w.dtype)],
+        scratch=[
+            pltpu.VMEM((2 * features, width), w.dtype),
+            pltpu.VMEM((rows, width), w.dtype),
+            pltpu.SemaphoreType.DMA((2,)),
+        ],
         flops=2 * work,
         moved=4_000_000,
+        place=HBM,
     )(grads, own_w, oth_w)
     return (grad_input, grad_weight)
 

time: 115 us -> 114 us (level)
  no operation moved by 1% of the time
where the time goes in v7:
time: 114 us
  blocking collectives  85 us (75%)
  starting transfers between devices  17.6 us (15%)
  Pallas kernels  5.88 us (5%)
  waiting for transfers between devices  2.93 us (3%)
  local copies, waits for them, and re-layouts  1.56 us (1%)
    all_to_all x1, blocking collectives, per_device(): code = lax.all_to_all(code, ('x', 'z'), 0, 0)  57.6 us
    all_to_all x1, blocking collectives, per_device(): grads = lax.all_to_all(copies, 'tensor', 0, 0)  27.5 us
    ppermute x1, starting transfers between devices, per_device(): got = lax.ppermute(oth, 'c', swap)  12.2 us
    ppermute x1, starting transfers between devices, per_device(): oth_w = lax.ppermute(own_w, 'c', swap)  5.42 us
  transfers between devices with their start and end apart: 2, of which 2 were waited for; matrix products, arithmetic and copies ran while one was open for 0% of the time, Pallas kernels for 1%

profile of v7, /device:TPU:1, one launch (start us, length us, event | category | flops | bytes accessed | tf_op | source)
XLA Modules:
  0.0 113.7 jit_solution(14322044562779381356)
XLA Ops:
  0.6 0.0 copy-start.1
  0.6 0.9 copy-done.1
  1.5 0.0 copy-start.3
  1.5 0.7 copy-done.3
  2.2 0.8 sort.1
  3.0 0.0 copy-start
  3.0 27.5 %all_to_all.10.g_ref = bf16[8,512,128]{2,1,0:T(8,128)(2,1)S(1)} all-to-all(bf16[8,512,128]{2,1,0:T(8,128)(2,1)S(1)} %sort.1), channel_id=1, replica_groups=mesh['z'=8,'x'=8,'c'=2,'tensor'=8] {'tensor'}, dimensions={0} | all-to-all | bytes 2097152 | tf_op jit(solution)/shard_map/all_to_all | solution.py:163
  30.5 0.0 copy-done
  30.5 0.7 weight_grads_other.1
  31.2 0.0 copy-start.2
  31.2 12.2 %collective-permute-start = (f32[512,640]{1,0:T(8,128)S(1)}, f32[512,640]{1,0:T(8,128)S(1)}, u32[]{:S(2)}, u32[]{:S(2)}) collective-permute-start(f32[512,640]{1,0:T(8,128)S(1)} %get-tuple-element.5), channel_id=1, source_target_pairs={{0,8},{8,0},{1,9},{9,1},{2,10},{10,2},{3,11},{11,3},{4,12},{12,4},... | collective-permute-start | bytes 3932168 | tf_op jit(solution)/shard_map/ppermute | solution.py:174
  43.4 0.6 weight_grads_own.1
  44.0 2.1 %collective-permute-done = f32[512,640]{1,0:T(8,128)S(1)} collective-permute-done((f32[512,640]{1,0:T(8,128)S(1)}, f32[512,640]{1,0:T(8,128)S(1)}, u32[]{:S(2)}, u32[]{:S(2)}) %collective-permute-start) | collective-permute-done | bytes 1310752 | tf_op jit(solution)/shard_map/ppermute | solution.py:174
  46.1 0.0 copy-done.2
  46.1 0.4 pack.1
  46.5 57.6 %all_to_all.11.in_ref = s16[64,8,1408]{2,1,0:T(8,128)(2,1)S(1)} all-to-all(s16[64,8,1408]{2,1,0:T(8,128)(2,1)S(1)} %pack.1), channel_id=1, replica_groups=mesh['z'=8,'x'=8,'c'=2,'tensor'=8] {'x','z'}, dimensions={0} | all-to-all | bytes 2883584 | tf_op jit(solution)/shard_map/all_to_all | solution.py:183
  104.0 0.7 unpack_weights.1
  104.8 5.4 %collective-permute-start.1 = (bf16[512,640]{1,0:T(8,128)(2,1)S(1)}, bf16[512,640]{1,0:T(8,128)(2,1)S(1)}, u32[]{:S(2)}, u32[]{:S(2)}) collective-permute-start(bf16[512,640]{1,0:T(8,128)(2,1)S(1)} %bitcast.5), channel_id=1, source_target_pairs={{0,8},{8,0},{1,9},{9,1},{2,10},{10,2},{3,11},{11,3},{4,12},{12,4},... | collective-permute-start | bytes 1966088 | tf_op jit(solution)/shard_map/ppermute | solution.py:186
  110.2 0.8 unpack_sum.1
  111.1 0.9 collective-permute-done.1.oth_ref
  111.9 1.8 %input_grads.1 = bf16[512,640]{1,0:T(8,128)(2,1)} custom-call(bf16[8,512,128]{2,1,0:T(8,128)(2,1)S(1)} %all_to_all.10.g_ref, bf16[512,640]{1,0:T(8,128)(2,1)S(1)} %bitcast.6, bf16[512,640]{1,0:T(8,128)(2,1)S(1)} %collective-permute-done.1.oth_ref), custom_call_target="tpu_custom_call" | custom-call | flops 671088640 | bytes 4000000 | tf_op jit(solution)/shard_map/input_grads/pallas_call | solution.py:191
Async XLA Ops:
  0.6 0.9 copy-start.1
  1.5 0.7 copy-start.3
  3.0 27.5 %copy-start = (bf16[512,640]{1,0:T(8,128)(2,1)S(1)}, bf16[512,640]{1,0:T(8,128)(2,1)}, u32[]{:S(2)}) copy-start(bf16[512,640]{1,0:T(8,128)(2,1)} %x_ref.3) | copy-start | bytes 1966084
  31.2 14.8 %copy-start.2 = (bf16[8,640]{1,0:T(8,128)(2,1)S(1)}, bf16[8,640]{1,0:T(8,128)(2,1)}, u32[]{:S(2)}) copy-start(bf16[8,640]{1,0:T(8,128)(2,1)} %w_ref.1) | copy-start | bytes 30724
  31.2 14.8 %collective-permute-start = (f32[512,640]{1,0:T(8,128)S(1)}, f32[512,640]{1,0:T(8,128)S(1)}, u32[]{:S(2)}, u32[]{:S(2)}) collective-permute-start(f32[512,640]{1,0:T(8,128)S(1)} %get-tuple-element.5), channel_id=1, source_target_pairs={{0,8},{8,0},{1,9},{9,1},{2,10},{10,2},{3,11},{11,3},{4,12},{12,4},... | collective-permute-start | bytes 3932168 | tf_op jit(solution)/shard_map/ppermute | solution.py:174
  104.8 7.1 %collective-permute-start.1 = (bf16[512,640]{1,0:T(8,128)(2,1)S(1)}, bf16[512,640]{1,0:T(8,128)(2,1)S(1)}, u32[]{:S(2)}, u32[]{:S(2)}) collective-permute-start(bf16[512,640]{1,0:T(8,128)(2,1)S(1)} %bitcast.5), channel_id=1, source_target_pairs={{0,8},{8,0},{1,9},{9,1},{2,10},{10,2},{3,11},{11,3},{4,12},{12,4},... | collective-permute-start | bytes 1966088 | tf_op jit(solution)/shard_map/ppermute | solution.py:186

commit v8 on v2

v8 whole, which is shorter than its diff:
```python
import functools
import math

import jax
import jax.numpy as jnp
from jax import lax
from jax.experimental import pallas as pl
from jax.experimental.pallas import tpu as pltpu
from jax.sharding import Mesh, PartitionSpec as P

STEPS = 256.0
LARGEST = 32767.0
BIAS = 127.0
VMEM = pl.BlockSpec(memory_space=pltpu.VMEM)
SMEM = pl.BlockSpec(memory_space=pltpu.SMEM)


def sort_kernel(place_ref, g_ref, out_ref):
    width = g_ref.shape[1]
    half = width // 2
    core = place_ref[0] % 2
    take = lax.broadcasted_iota(jnp.int32, (width, width), 0)
    place = lax.broadcasted_iota(jnp.int32, (width, width), 1)
    inner = place % half
    kind = jnp.where(place < half, core, 1 - core)
    order = jnp.where(take == (inner // 8) * 16 + inner % 8 + 8 * kind, 1.0, 0.0).astype(g_ref.dtype)
    g = jnp.dot(g_ref[...], order, preferred_element_type=jnp.float32).astype(out_ref.dtype)
    for k in range(out_ref.shape[0]):
        out_ref[k] = g


def other_kernel(lengths_ref, place_ref, g_ref, x_ref, sum_ref, own_ref, oth_ref, live_ref):
    blocks, rows, width = g_ref.shape
    half = width // 2
    live = lax.broadcasted_iota(jnp.int32, x_ref.shape, 0) < lengths_ref[place_ref[0]]
    live_ref[...] = jnp.where(live, x_ref[...].astype(jnp.float32), 0.0).astype(x_ref.dtype)
    for k in range(blocks):
        turned = g_ref[k].T
        own_ref[k * half : (k + 1) * half, :] = turned[:half]
        oth_ref[k * half : (k + 1) * half, :] = turned[half:]
    sum_ref[...] = jnp.dot(oth_ref[...], live_ref[...], preferred_element_type=jnp.float32)


def own_kernel(g_ref, x_ref, out_ref):
    out_ref[...] = jnp.dot(g_ref[...], x_ref[...], preferred_element_type=jnp.float32)


def turned_place(k, lines, line):
    return k % line * lines + k // line


def pack_kernel(line, a_ref, b_ref, w_ref, out_ref):
    rows, width = w_ref.shape
    lanes = out_ref.shape[2] - 2 * width

    def store(k, at, v):
        out_ref[k, :, at : at + v.shape[1]] = v.astype(jnp.int32).astype(out_ref.dtype)

    w = w_ref[...].astype(jnp.float32)
    size = jnp.abs(w)
    e = jnp.floor(jnp.log2(jnp.maximum(size, 2.0**-126)))
    bits = (e + BIAS) * 128.0 + (size * jnp.exp2(-e) * 128.0 - 128.0)
    bits = jnp.where(size < 2.0**-126, 0.0, bits)
    bits = jnp.round(jnp.where(w < 0.0, -bits, bits))
    for s in range(out_ref.shape[0]):
        k = turned_place(s, out_ref.shape[0] // line, line)
        v = a_ref[s] + b_ref[s]
        top = jnp.maximum(jnp.max(jnp.abs(v), axis=1, keepdims=True), 1e-30)
        e = jnp.ceil(STEPS * jnp.log2(top * (1.0 / LARGEST))) + 1.0
        store(k, 0, jnp.round(v * jnp.exp2(e * (-1.0 / STEPS))))
        store(k, width, jnp.broadcast_to(e, (rows, lanes)))
        store(k, width + lanes, bits)


def weights_kernel(line, in_ref, out_ref):
    width = out_ref.shape[2]
    for k in range(in_ref.shape[0]):
        s = turned_place(k, in_ref.shape[0] // line, line)
        bits = in_ref[s, :, in_ref.shape[2] - width :].astype(jnp.int32)
        size = jnp.abs(bits)
        e = (size >> 7).astype(jnp.float32) - BIAS
        v = ((size & 127) + 128).astype(jnp.float32) * jnp.exp2(e) * (1.0 / 128.0)
        v = jnp.where(size < 128, 0.0, jnp.where(bits < 0, -v, v))
        out_ref[k] = v.astype(out_ref.dtype)


def sum_kernel(scale, in_ref, out_ref):
    rows, width = out_ref.shape
    lanes = in_ref.shape[2] - 2 * width
    total = [jnp.zeros((rows, lanes), jnp.float32) for _ in range(width // lanes)]
    for s in range(in_ref.shape[0]):
        step = jnp.exp2(in_ref[s, :, width : width + lanes].astype(jnp.int32).astype(jnp.float32) * (1.0 / STEPS))
        for t in range(width // lanes):
            q = in_ref[s, :, t * lanes : (t + 1) * lanes].astype(jnp.int32).astype(jnp.float32)
            total[t] = total[t] + q * step
    for t in range(width // lanes):
        out_ref[:, t * lanes : (t + 1) * lanes] = total[t] * scale


def turned_dot(g, w):
    return lax.dot_general(g, w, (((0,), (0,)), ((), ())), preferred_element_type=jnp.float32)


def first_kernel(g_ref, w_ref, out_ref):
    out_ref[...] = turned_dot(g_ref[...], w_ref[...])


def input_kernel(lengths_ref, place_ref, part_ref, g_ref, w_ref, out_ref):
    live = lax.broadcasted_iota(jnp.int32, out_ref.shape, 0) < lengths_ref[place_ref[0]]
    total = part_ref[...] + turned_dot(g_ref[...], w_ref[...])
    out_ref[...] = jnp.where(live, total, 0.0).astype(out_ref.dtype)


def call(kernel, out, specs, name, scratch=(), flops=0, moved=0):
    return pl.pallas_call(
        kernel,
        out_shape=[jax.ShapeDtypeStruct(*o) for o in out],
        in_specs=specs,
        out_specs=[VMEM] * len(out),
        scratch_shapes=scratch,
        compiler_params=pltpu.CompilerParams(vmem_limit_bytes=14 * 1024 * 1024),
        cost_estimate=pl.CostEstimate(flops=flops, bytes_accessed=moved, transcendentals=0),
        name=name,
    )


def per_device(nz, nx, ny, x, g, w, lengths):
    rows, width = x.shape
    block = g.shape[1]
    half = block // 2
    features = ny * half
    lanes = 128
    work = 2 * rows * features * width
    group = (lax.axis_index("z") * nx + lax.axis_index("x")) * 2 + lax.axis_index("c")
    swap = [(0, 1), (1, 0)]

    place = group.astype(jnp.int32).reshape(1)
    (copies,) = call(sort_kernel, [((ny, rows, block), g.dtype)], [SMEM, VMEM], "sort", moved=2_000_000)(place, g)
    grads = lax.all_to_all(copies, "tensor", 0, 0)

    turned = ((features, rows), g.dtype)
    oth, own_g, oth_g, live_x = call(
        other_kernel,
        [((features, width), jnp.float32), turned, turned, (x.shape, x.dtype)],
        [SMEM, SMEM, VMEM, VMEM],
        "weight_grads_other",
        flops=work,
        moved=3_000_000,
    )(lengths, place, grads, x)
    got = lax.ppermute(oth, "c", swap)
    (mine,) = call(
        own_kernel, [((features, width), jnp.float32)], [VMEM, VMEM], "weight_grads_own", flops=work, moved=3_000_000
    )(own_g, live_x)

    peers = nz * nx
    (code,) = call(functools.partial(pack_kernel, nx), [((peers, 8, 2 * width + lanes), jnp.int16)], [VMEM] * 3, "pack", moved=4_000_000)(
        mine.reshape(peers, 8, width), got.reshape(peers, 8, width), w
    )
    code = lax.all_to_all(code, ("x", "z"), 0, 0)
    (own_w,) = call(functools.partial(weights_kernel, nx), [((peers, 8, width), w.dtype)], [VMEM], "unpack_weights", moved=1_500_000)(code)
    own_w = own_w.reshape(features, width)
    oth_w = lax.ppermute(own_w, "c", swap)
    scale = 1.0 / math.sqrt(rows * peers * 2)
    (grad_weight,) = call(
        functools.partial(sum_kernel, scale), [((8, width), jnp.float32)], [VMEM], "unpack_sum", moved=1_000_000
    )(code)
    (part,) = call(
        first_kernel, [((rows, width), jnp.float32)], [VMEM] * 2, "input_grads_own", flops=work, moved=3_000_000
    )(own_g, own_w)
    (grad_input,) = call(
        input_kernel,
        [((rows, width), jnp.bfloat16)],
        [SMEM, SMEM, VMEM, VMEM, VMEM],
        "input_grads",
        flops=work,
        moved=4_000_000,
    )(lengths, place, part, oth_g, oth_w)
    return (grad_input, grad_weight)


def solution(mesh):
    dp, ny = mesh.shape["dp"], mesh.shape["tensor"]
    nz, nx = ny, dp // (2 * ny)
    fine = Mesh(mesh.devices.reshape(nz, nx, 2, ny), ("z", "x", "c", "tensor"))
    both = P(("z", "x", "c"), "tensor")
    return jax.shard_map(
        functools.partial(per_device, nz, nx, ny),
        mesh=fine,
        in_specs=(both, both, both, P()),
        out_specs=(both, both),
        check_vma=False,
    )
```

time: 115 us -> 114 us (level)
    pallas_call x5 -> x6, Pallas kernels: 4.52 us -> 5.29 us  [the longest x1 1.99 us: per_device(): call(input_kernel, [((rows, width), jnp.bfloat16)], [SMEM, SMEM, VMEM, VM...]
  transfers between devices with their start and end apart: 2 -> 2, of which waited for: 2 -> 2; matrix products, arithmetic and copies ran while one was open for 0% -> 0% of each run, Pallas kernels for 1% -> 2%
where the time goes in v8:
time: 114 us; the launch traced here: 113 us
  blocking collectives  85 us (75%)
  starting transfers between devices  17.6 us (15%)
  Pallas kernels  6.7 us (6%)
  waiting for transfers between devices  2.32 us (2%)
    all_to_all x1, blocking collectives, per_device(): code = lax.all_to_all(code, ('x', 'z'), 0, 0)  57.5 us
    all_to_all x1, blocking collectives, per_device(): grads = lax.all_to_all(copies, 'tensor', 0, 0)  27.5 us
    ppermute x1, starting transfers between devices, per_device(): got = lax.ppermute(oth, 'c', swap)  12.2 us
    ppermute x1, starting transfers between devices, per_device(): oth_w = lax.ppermute(own_w, 'c', swap)  5.42 us
  transfers between devices with their start and end apart: 2, of which 2 were waited for; matrix products, arithmetic and copies ran while one was open for 0% of the time, Pallas kernels for 2%

profile of v8, /device:TPU:1, one launch (start us, length us, event | category | flops | bytes accessed | tf_op | source)
XLA Modules:
  0.0 113.2 jit_solution(8495941486981258264)
XLA Ops:
  0.6 0.0 copy-start.1
  0.6 0.9 copy-done.1
  1.5 0.2 sort.1
  1.8 0.0 copy-start
  1.8 0.0 copy-start.3
  1.8 27.5 %all_to_all.10.g_ref = bf16[8,512,128]{2,1,0:T(8,128)(2,1)S(1)} all-to-all(bf16[8,512,128]{2,1,0:T(8,128)(2,1)S(1)} %sort.1), channel_id=1, replica_groups=mesh['z'=8,'x'=8,'c'=2,'tensor'=8] {'tensor'}, dimensions={0} | all-to-all | bytes 2097152 | tf_op jit(solution)/shard_map/all_to_all | solution.py:139
  29.3 0.0 copy-done
  29.3 0.0 copy-done.3
  29.3 1.3 %weight_grads_other.1 = (f32[512,640]{1,0:T(8,128)S(1)}, bf16[512,512]{1,0:T(8,128)(2,1)S(1)}, bf16[512,512]{1,0:T(8,128)(2,1)S(1)}, bf16[512,640]{1,0:T(8,128)(2,1)S(1)}) custom-call(s32[128]{0:T(128)S(1)} %copy-done.3, s32[1]{0:T(128)} %bitcast.place_ref, bf16[8,512,128]{2,1,0:T(8,128)(2,1)S(1)} %all_to_all.10.g_ref, bf16[512,640]{1,0:T(8,128)(2,1)S(1)} %copy-done), custom_call_target="tpu_custom_call" | custom-call | flops 335544320 | bytes 3000000 | tf_op jit(solution)/shard_map/weight_grads_other/pallas_call | solution.py:142
  30.6 0.0 copy-start.2
  30.6 12.2 %collective-permute-start = (f32[512,640]{1,0:T(8,128)S(1)}, f32[512,640]{1,0:T(8,128)S(1)}, u32[]{:S(2)}, u32[]{:S(2)}) collective-permute-start(f32[512,640]{1,0:T(8,128)S(1)} %get-tuple-element.8), channel_id=1, source_target_pairs={{0,8},{8,0},{1,9},{9,1},{2,10},{10,2},{3,11},{11,3},{4,12},{12,4},... | collective-permute-start | bytes 3932168 | tf_op jit(solution)/shard_map/ppermute | solution.py:150
  42.8 0.6 weight_grads_own.1
  43.4 2.1 %collective-permute-done = f32[512,640]{1,0:T(8,128)S(1)} collective-permute-done((f32[512,640]{1,0:T(8,128)S(1)}, f32[512,640]{1,0:T(8,128)S(1)}, u32[]{:S(2)}, u32[]{:S(2)}) %collective-permute-start) | collective-permute-done | bytes 1310752 | tf_op jit(solution)/shard_map/ppermute | solution.py:150
  45.4 0.0 copy-done.2
  45.4 0.4 pack.1
  45.8 57.5 %all_to_all.11.in_ref = s16[64,8,1408]{2,1,0:T(8,128)(2,1)S(1)} all-to-all(s16[64,8,1408]{2,1,0:T(8,128)(2,1)S(1)} %pack.1), channel_id=1, replica_groups=mesh['z'=8,'x'=8,'c'=2,'tensor'=8] {'x','z'}, dimensions={0} | all-to-all | bytes 2883584 | tf_op jit(solution)/shard_map/all_to_all | solution.py:159
  103.3 0.7 unpack_weights.1
  104.1 5.4 %collective-permute-start.1 = (bf16[512,640]{1,0:T(8,128)(2,1)S(1)}, bf16[512,640]{1,0:T(8,128)(2,1)S(1)}, u32[]{:S(2)}, u32[]{:S(2)}) collective-permute-start(bf16[512,640]{1,0:T(8,128)(2,1)S(1)} %bitcast.5), channel_id=1, source_target_pairs={{0,8},{8,0},{1,9},{9,1},{2,10},{10,2},{3,11},{11,3},{4,12},{12,4},... | collective-permute-start | bytes 1966088 | tf_op jit(solution)/shard_map/ppermute | solution.py:162
  109.5 0.8 unpack_sum.1
  110.4 0.6 input_grads_own.1.part_ref
  111.0 0.3 collective-permute-done.1.w_ref
  111.2 2.0 %input_grads.1 = bf16[512,640]{1,0:T(8,128)(2,1)} custom-call(s32[128]{0:T(128)S(1)} %copy-done.3, s32[1]{0:T(128)} %bitcast.place_ref, f32[512,640]{1,0:T(8,128)S(1)} %input_grads_own.1.part_ref, bf16[512,512]{1,0:T(8,128)(2,1)S(1)} %get-tuple-element.9.g_ref, bf16[512,640]{1,0:T(8,128)(2,1)S(1)} %collective-permute-done.1.w_ref), custom_call_target="tpu_custom_call" | custom-call | flops 335544320 | bytes 4000000 | tf_op jit(solution)/shard_map/input_grads/pallas_call | solution.py:170
Async XLA Ops:
  0.6 0.9 copy-start.1
  1.8 27.5 %copy-start = (bf16[512,640]{1,0:T(8,128)(2,1)S(1)}, bf16[512,640]{1,0:T(8,128)(2,1)}, u32[]{:S(2)}) copy-start(bf16[512,640]{1,0:T(8,128)(2,1)} %x_ref.1) | copy-start | bytes 1966084
  1.8 27.5 %copy-start.3 = (s32[128]{0:T(128)S(1)}, s32[128]{0:T(128)}, u32[]{:S(2)}) copy-start(s32[128]{0:T(128)} %lengths_ref.3) | copy-start | bytes 1540
  30.6 14.8 %copy-start.2 = (bf16[8,640]{1,0:T(8,128)(2,1)S(1)}, bf16[8,640]{1,0:T(8,128)(2,1)}, u32[]{:S(2)}) copy-start(bf16[8,640]{1,0:T(8,128)(2,1)} %w_ref.1) | copy-start | bytes 30724
  30.6 14.8 %collective-permute-start = (f32[512,640]{1,0:T(8,128)S(1)}, f32[512,640]{1,0:T(8,128)S(1)}, u32[]{:S(2)}, u32[]{:S(2)}) collective-permute-start(f32[512,640]{1,0:T(8,128)S(1)} %get-tuple-element.8), channel_id=1, source_target_pairs={{0,8},{8,0},{1,9},{9,1},{2,10},{10,2},{3,11},{11,3},{4,12},{12,4},... | collective-permute-start | bytes 3932168 | tf_op jit(solution)/shard_map/ppermute | solution.py:150
  104.1 7.1 %collective-permute-start.1 = (bf16[512,640]{1,0:T(8,128)(2,1)S(1)}, bf16[512,640]{1,0:T(8,128)(2,1)S(1)}, u32[]{:S(2)}, u32[]{:S(2)}) collective-permute-start(bf16[512,640]{1,0:T(8,128)(2,1)S(1)} %bitcast.5), channel_id=1, source_target_pairs={{0,8},{8,0},{1,9},{9,1},{2,10},{10,2},{3,11},{11,3},{4,12},{12,4},... | collective-permute-start | bytes 1966088 | tf_op jit(solution)/shard_map/ppermute | solution.py:162

commit v9 on v8

--- a/solution.py
+++ b/solution.py
@@ -12,6 +12,7 @@
 LARGEST = 32767.0
 BIAS = 127.0
 VMEM = pl.BlockSpec(memory_space=pltpu.VMEM)
+HBM = pl.BlockSpec(memory_space=pltpu.HBM)
 SMEM = pl.BlockSpec(memory_space=pltpu.SMEM)
 
 
@@ -41,8 +42,10 @@
     sum_ref[...] = jnp.dot(oth_ref[...], live_ref[...], preferred_element_type=jnp.float32)
 
 
-def own_kernel(g_ref, x_ref, out_ref):
-    out_ref[...] = jnp.dot(g_ref[...], x_ref[...], preferred_element_type=jnp.float32)
+def own_kernel(own_ref, oth_ref, x_ref, sum_ref, own_back_ref, oth_back_ref):
+    sum_ref[...] = jnp.dot(own_ref[...], x_ref[...], preferred_element_type=jnp.float32)
+    own_back_ref[...] = own_ref[...].T
+    oth_back_ref[...] = oth_ref[...].T
 
 
 def turned_place(k, lines, line):
@@ -97,26 +100,31 @@
         out_ref[:, t * lanes : (t + 1) * lanes] = total[t] * scale
 
 
-def turned_dot(g, w):
-    return lax.dot_general(g, w, (((0,), (0,)), ((), ())), preferred_element_type=jnp.float32)
-
-
 def first_kernel(g_ref, w_ref, out_ref):
-    out_ref[...] = turned_dot(g_ref[...], w_ref[...])
-
-
-def input_kernel(lengths_ref, place_ref, part_ref, g_ref, w_ref, out_ref):
-    live = lax.broadcasted_iota(jnp.int32, out_ref.shape, 0) < lengths_ref[place_ref[0]]
-    total = part_ref[...] + turned_dot(g_ref[...], w_ref[...])
-    out_ref[...] = jnp.where(live, total, 0.0).astype(out_ref.dtype)
-
-
-def call(kernel, out, specs, name, scratch=(), flops=0, moved=0):
+    out_ref[...] = jnp.dot(g_ref[...], w_ref[...], preferred_element_type=jnp.float32)
+
+
+def input_kernel(lengths_ref, place_ref, part_ref, g_ref, w_ref, out_ref, held_ref, sems):
+    length = lengths_ref[place_ref[0]]
+    size = out_ref.shape[0] // sems.shape[0]
+    copies = []
+    for i in range(sems.shape[0]):
+        at = slice(i * size, (i + 1) * size)
+        total = part_ref[at, :] + jnp.dot(g_ref[at, :], w_ref[...], preferred_element_type=jnp.float32)
+        live = lax.broadcasted_iota(jnp.int32, total.shape, 0) + i * size < length
+        held_ref[at, :] = jnp.where(live, total, 0.0).astype(out_ref.dtype)
+        copies.append(pltpu.make_async_copy(held_ref.at[at], out_ref.at[at], sems.at[i]))
+        copies[-1].start()
+    for copy in copies:
+        copy.wait()
+
+
+def call(kernel, out, specs, name, scratch=(), flops=0, moved=0, place=VMEM):
     return pl.pallas_call(
         kernel,
         out_shape=[jax.ShapeDtypeStruct(*o) for o in out],
         in_specs=specs,
-        out_specs=[VMEM] * len(out),
+        out_specs=[place] * len(out),
         scratch_shapes=scratch,
         compiler_params=pltpu.CompilerParams(vmem_limit_bytes=14 * 1024 * 1024),
         cost_estimate=pl.CostEstimate(flops=flops, bytes_accessed=moved, transcendentals=0),
@@ -148,9 +156,15 @@
         moved=3_000_000,
     )(lengths, place, grads, x)
     got = lax.ppermute(oth, "c", swap)
-    (mine,) = call(
-        own_kernel, [((features, width), jnp.float32)], [VMEM, VMEM], "weight_grads_own", flops=work, moved=3_000_000
-    )(own_g, live_x)
+    back = ((rows, features), g.dtype)
+    mine, own_g, oth_g = call(
+        own_kernel,
+        [((features, width), jnp.float32), back, back],
+        [VMEM] * 3,
+        "weight_grads_own",
+        flops=work,
+        moved=3_000_000,
+    )(own_g, oth_g, live_x)
 
     peers = nz * nx
     (code,) = call(functools.partial(pack_kernel, nx), [((peers, 8, 2 * width + lanes), jnp.int16)], [VMEM] * 3, "pack", moved=4_000_000)(
@@ -172,8 +186,10 @@
         [((rows, width), jnp.bfloat16)],
         [SMEM, SMEM, VMEM, VMEM, VMEM],
         "input_grads",
+        scratch=[pltpu.VMEM((rows, width), w.dtype), pltpu.SemaphoreType.DMA((4,))],
         flops=work,
         moved=4_000_000,
+        place=HBM,
     )(lengths, place, part, oth_g, oth_w)
     return (grad_input, grad_weight)
 

time: 114 us -> 113 us (level)
  no operation moved by 1% of the time
where the time goes in v9:
time: 113 us
  blocking collectives  85 us (75%)
  starting transfers between devices  17.6 us (16%)
  Pallas kernels  6.5 us (6%)
  waiting for transfers between devices  2.35 us (2%)
    all_to_all x1, blocking collectives, per_device(): code = lax.all_to_all(code, ('x', 'z'), 0, 0)  57.5 us
    all_to_all x1, blocking collectives, per_device(): grads = lax.all_to_all(copies, 'tensor', 0, 0)  27.5 us
    ppermute x1, starting transfers between devices, per_device(): got = lax.ppermute(oth, 'c', swap)  12.2 us
    ppermute x1, starting transfers between devices, per_device(): oth_w = lax.ppermute(own_w, 'c', swap)  5.42 us
  transfers between devices with their start and end apart: 2, of which 2 were waited for; matrix products, arithmetic and copies ran while one was open for 0% of the time, Pallas kernels for 2%

profile of v9, /device:TPU:1, one launch (start us, length us, event | category | flops | bytes accessed | tf_op | source)
XLA Modules:
  0.0 113.0 jit_solution(17931021503924367893)
XLA Ops:
  0.6 0.0 copy-start.1
  0.6 0.9 copy-done.1
  1.5 0.2 sort.1
  1.8 0.0 copy-start
  1.8 0.0 copy-start.3
  1.8 27.5 %all_to_all.10.g_ref = bf16[8,512,128]{2,1,0:T(8,128)(2,1)S(1)} all-to-all(bf16[8,512,128]{2,1,0:T(8,128)(2,1)S(1)} %sort.1), channel_id=1, replica_groups=mesh['z'=8,'x'=8,'c'=2,'tensor'=8] {'tensor'}, dimensions={0} | all-to-all | bytes 2097152 | tf_op jit(solution)/shard_map/all_to_all | solution.py:147
  29.3 0.0 copy-done
  29.3 0.0 copy-done.3
  29.3 0.0 copy-start.2
  29.3 1.3 %weight_grads_other.1 = (f32[512,640]{1,0:T(8,128)S(1)}, bf16[512,512]{1,0:T(8,128)(2,1)S(1)}, bf16[512,512]{1,0:T(8,128)(2,1)S(1)}, bf16[512,640]{1,0:T(8,128)(2,1)S(1)}) custom-call(s32[128]{0:T(128)S(1)} %copy-done.3, s32[1]{0:T(128)} %bitcast.place_ref, bf16[8,512,128]{2,1,0:T(8,128)(2,1)S(1)} %all_to_all.10.g_ref, bf16[512,640]{1,0:T(8,128)(2,1)S(1)} %copy-done), custom_call_target="tpu_custom_call" | custom-call | flops 335544320 | bytes 3000000 | tf_op jit(solution)/shard_map/weight_grads_other/pallas_call | solution.py:150
  30.6 12.2 %collective-permute-start = (f32[512,640]{1,0:T(8,128)S(1)}, f32[512,640]{1,0:T(8,128)S(1)}, u32[]{:S(2)}, u32[]{:S(2)}) collective-permute-start(f32[512,640]{1,0:T(8,128)S(1)} %get-tuple-element.14), channel_id=1, source_target_pairs={{0,8},{8,0},{1,9},{9,1},{2,10},{10,2},{3,11},{11,3},{4,12},{12,4},... | collective-permute-start | bytes 3932168 | tf_op jit(solution)/shard_map/ppermute | solution.py:158
  42.8 0.6 weight_grads_own.1
  43.4 2.1 %collective-permute-done = f32[512,640]{1,0:T(8,128)S(1)} collective-permute-done((f32[512,640]{1,0:T(8,128)S(1)}, f32[512,640]{1,0:T(8,128)S(1)}, u32[]{:S(2)}, u32[]{:S(2)}) %collective-permute-start) | collective-permute-done | bytes 1310752 | tf_op jit(solution)/shard_map/ppermute | solution.py:158
  45.4 0.0 copy-done.2
  45.4 0.4 pack.1
  45.8 57.5 %all_to_all.11.in_ref = s16[64,8,1408]{2,1,0:T(8,128)(2,1)S(1)} all-to-all(s16[64,8,1408]{2,1,0:T(8,128)(2,1)S(1)} %pack.1), channel_id=1, replica_groups=mesh['z'=8,'x'=8,'c'=2,'tensor'=8] {'x','z'}, dimensions={0} | all-to-all | bytes 2883584 | tf_op jit(solution)/shard_map/all_to_all | solution.py:173
  103.3 0.7 unpack_weights.1
  104.1 5.4 %collective-permute-start.1 = (bf16[512,640]{1,0:T(8,128)(2,1)S(1)}, bf16[512,640]{1,0:T(8,128)(2,1)S(1)}, u32[]{:S(2)}, u32[]{:S(2)}) collective-permute-start(bf16[512,640]{1,0:T(8,128)(2,1)S(1)} %bitcast.4), channel_id=1, source_target_pairs={{0,8},{8,0},{1,9},{9,1},{2,10},{10,2},{3,11},{11,3},{4,12},{12,4},... | collective-permute-start | bytes 1966088 | tf_op jit(solution)/shard_map/ppermute | solution.py:176
  109.5 0.8 unpack_sum.1
  110.4 0.6 input_grads_own.1.part_ref
  110.9 0.3 collective-permute-done.1.w_ref
  111.2 1.8 %input_grads.1 = bf16[512,640]{1,0:T(8,128)(2,1)} custom-call(s32[128]{0:T(128)S(1)} %copy-done.3, s32[1]{0:T(128)} %bitcast.place_ref, f32[512,640]{1,0:T(8,128)S(1)} %input_grads_own.1.part_ref, bf16[512,512]{1,0:T(8,128)(2,1)S(1)} %get-tuple-element.15.g_ref, bf16[512,640]{1,0:T(8,128)(2,1)S(1)} %collective-permute-done.1.w_ref), custom_call_target="tpu_custom_call" | custom-call | flops 335544320 | bytes 4000000 | tf_op jit(solution)/shard_map/input_grads/pallas_call | solution.py:184
Async XLA Ops:
  0.6 0.9 copy-start.1
  1.8 27.5 %copy-start = (bf16[512,640]{1,0:T(8,128)(2,1)S(1)}, bf16[512,640]{1,0:T(8,128)(2,1)}, u32[]{:S(2)}) copy-start(bf16[512,640]{1,0:T(8,128)(2,1)} %x_ref.1) | copy-start | bytes 1966084
  1.8 27.5 %copy-start.3 = (s32[128]{0:T(128)S(1)}, s32[128]{0:T(128)}, u32[]{:S(2)}) copy-start(s32[128]{0:T(128)} %lengths_ref.3) | copy-start | bytes 1540
  29.3 16.1 %copy-start.2 = (bf16[8,640]{1,0:T(8,128)(2,1)S(1)}, bf16[8,640]{1,0:T(8,128)(2,1)}, u32[]{:S(2)}) copy-start(bf16[8,640]{1,0:T(8,128)(2,1)} %w_ref.1) | copy-start | bytes 30724
  30.6 14.8 %collective-permute-start = (f32[512,640]{1,0:T(8,128)S(1)}, f32[512,640]{1,0:T(8,128)S(1)}, u32[]{:S(2)}, u32[]{:S(2)}) collective-permute-start(f32[512,640]{1,0:T(8,128)S(1)} %get-tuple-element.14), channel_id=1, source_target_pairs={{0,8},{8,0},{1,9},{9,1},{2,10},{10,2},{3,11},{11,3},{4,12},{12,4},... | collective-permute-start | bytes 3932168 | tf_op jit(solution)/shard_map/ppermute | solution.py:158
  104.1 7.1 %collective-permute-start.1 = (bf16[512,640]{1,0:T(8,128)(2,1)S(1)}, bf16[512,640]{1,0:T(8,128)(2,1)S(1)}, u32[]{:S(2)}, u32[]{:S(2)}) collective-permute-start(bf16[512,640]{1,0:T(8,128)(2,1)S(1)} %bitcast.4), channel_id=1, source_target_pairs={{0,8},{8,0},{1,9},{9,1},{2,10},{10,2},{3,11},{11,3},{4,12},{12,4},... | collective-permute-start | bytes 1966088 | tf_op jit(solution)/shard_map/ppermute | solution.py:176

commit v10 on v9

--- a/solution.py
+++ b/solution.py
@@ -186,7 +186,7 @@
         [((rows, width), jnp.bfloat16)],
         [SMEM, SMEM, VMEM, VMEM, VMEM],
         "input_grads",
-        scratch=[pltpu.VMEM((rows, width), w.dtype), pltpu.SemaphoreType.DMA((4,))],
+        scratch=[pltpu.VMEM((rows, width), w.dtype), pltpu.SemaphoreType.DMA((2,))],
         flops=work,
         moved=4_000_000,
         place=HBM,

time: 113 us -> 113 us (level)
  no operation moved by 1% of the time
where the time goes in v10:
time: 113 us
  blocking collectives  85 us (75%)
  starting transfers between devices  17.6 us (16%)
  Pallas kernels  6.53 us (6%)
  waiting for transfers between devices  2.35 us (2%)
    all_to_all x1, blocking collectives, per_device(): code = lax.all_to_all(code, ('x', 'z'), 0, 0)  57.5 us
    all_to_all x1, blocking collectives, per_device(): grads = lax.all_to_all(copies, 'tensor', 0, 0)  27.5 us
    ppermute x1, starting transfers between devices, per_device(): got = lax.ppermute(oth, 'c', swap)  12.2 us
    ppermute x1, starting transfers between devices, per_device(): oth_w = lax.ppermute(own_w, 'c', swap)  5.42 us
  transfers between devices with their start and end apart: 2, of which 2 were waited for; matrix products, arithmetic and copies ran while one was open for 0% of the time, Pallas kernels for 2%

profile of v10, /device:TPU:1, one launch (start us, length us, event | category | flops | bytes accessed | tf_op | source)
XLA Modules:
  0.0 113.1 jit_solution(5456812022384583837)
XLA Ops:
  0.6 0.0 copy-start.1
  0.6 0.9 copy-done.1
  1.5 0.2 sort.1
  1.8 0.0 copy-start
  1.8 0.0 copy-start.3
  1.8 27.5 %all_to_all.10.g_ref = bf16[8,512,128]{2,1,0:T(8,128)(2,1)S(1)} all-to-all(bf16[8,512,128]{2,1,0:T(8,128)(2,1)S(1)} %sort.1), channel_id=1, replica_groups=mesh['z'=8,'x'=8,'c'=2,'tensor'=8] {'tensor'}, dimensions={0} | all-to-all | bytes 2097152 | tf_op jit(solution)/shard_map/all_to_all | solution.py:147
  29.3 0.0 copy-done
  29.3 0.0 copy-done.3
  29.3 0.0 copy-start.2
  29.3 1.3 %weight_grads_other.1 = (f32[512,640]{1,0:T(8,128)S(1)}, bf16[512,512]{1,0:T(8,128)(2,1)S(1)}, bf16[512,512]{1,0:T(8,128)(2,1)S(1)}, bf16[512,640]{1,0:T(8,128)(2,1)S(1)}) custom-call(s32[128]{0:T(128)S(1)} %copy-done.3, s32[1]{0:T(128)} %bitcast.place_ref, bf16[8,512,128]{2,1,0:T(8,128)(2,1)S(1)} %all_to_all.10.g_ref, bf16[512,640]{1,0:T(8,128)(2,1)S(1)} %copy-done), custom_call_target="tpu_custom_call" | custom-call | flops 335544320 | bytes 3000000 | tf_op jit(solution)/shard_map/weight_grads_other/pallas_call | solution.py:150
  30.6 12.2 %collective-permute-start = (f32[512,640]{1,0:T(8,128)S(1)}, f32[512,640]{1,0:T(8,128)S(1)}, u32[]{:S(2)}, u32[]{:S(2)}) collective-permute-start(f32[512,640]{1,0:T(8,128)S(1)} %get-tuple-element.14), channel_id=1, source_target_pairs={{0,8},{8,0},{1,9},{9,1},{2,10},{10,2},{3,11},{11,3},{4,12},{12,4},... | collective-permute-start | bytes 3932168 | tf_op jit(solution)/shard_map/ppermute | solution.py:158
  42.8 0.6 weight_grads_own.1
  43.4 2.1 %collective-permute-done = f32[512,640]{1,0:T(8,128)S(1)} collective-permute-done((f32[512,640]{1,0:T(8,128)S(1)}, f32[512,640]{1,0:T(8,128)S(1)}, u32[]{:S(2)}, u32[]{:S(2)}) %collective-permute-start) | collective-permute-done | bytes 1310752 | tf_op jit(solution)/shard_map/ppermute | solution.py:158
  45.4 0.0 copy-done.2
  45.4 0.4 pack.1
  45.8 57.5 %all_to_all.11.in_ref = s16[64,8,1408]{2,1,0:T(8,128)(2,1)S(1)} all-to-all(s16[64,8,1408]{2,1,0:T(8,128)(2,1)S(1)} %pack.1), channel_id=1, replica_groups=mesh['z'=8,'x'=8,'c'=2,'tensor'=8] {'x','z'}, dimensions={0} | all-to-all | bytes 2883584 | tf_op jit(solution)/shard_map/all_to_all | solution.py:173
  103.3 0.7 unpack_weights.1
  104.1 5.4 %collective-permute-start.1 = (bf16[512,640]{1,0:T(8,128)(2,1)S(1)}, bf16[512,640]{1,0:T(8,128)(2,1)S(1)}, u32[]{:S(2)}, u32[]{:S(2)}) collective-permute-start(bf16[512,640]{1,0:T(8,128)(2,1)S(1)} %bitcast.4), channel_id=1, source_target_pairs={{0,8},{8,0},{1,9},{9,1},{2,10},{10,2},{3,11},{11,3},{4,12},{12,4},... | collective-permute-start | bytes 1966088 | tf_op jit(solution)/shard_map/ppermute | solution.py:176
  109.5 0.8 unpack_sum.1
  110.4 0.6 input_grads_own.1.part_ref
  110.9 0.3 collective-permute-done.1.w_ref
  111.2 1.9 %input_grads.1 = bf16[512,640]{1,0:T(8,128)(2,1)} custom-call(s32[128]{0:T(128)S(1)} %copy-done.3, s32[1]{0:T(128)} %bitcast.place_ref, f32[512,640]{1,0:T(8,128)S(1)} %input_grads_own.1.part_ref, bf16[512,512]{1,0:T(8,128)(2,1)S(1)} %get-tuple-element.15.g_ref, bf16[512,640]{1,0:T(8,128)(2,1)S(1)} %collective-permute-done.1.w_ref), custom_call_target="tpu_custom_call" | custom-call | flops 335544320 | bytes 4000000 | tf_op jit(solution)/shard_map/input_grads/pallas_call | solution.py:184
Async XLA Ops:
  0.6 0.9 copy-start.1
  1.8 27.5 %copy-start = (bf16[512,640]{1,0:T(8,128)(2,1)S(1)}, bf16[512,640]{1,0:T(8,128)(2,1)}, u32[]{:S(2)}) copy-start(bf16[512,640]{1,0:T(8,128)(2,1)} %x_ref.1) | copy-start | bytes 1966084
  1.8 27.5 %copy-start.3 = (s32[128]{0:T(128)S(1)}, s32[128]{0:T(128)}, u32[]{:S(2)}) copy-start(s32[128]{0:T(128)} %lengths_ref.3) | copy-start | bytes 1540
  29.3 16.1 %copy-start.2 = (bf16[8,640]{1,0:T(8,128)(2,1)S(1)}, bf16[8,640]{1,0:T(8,128)(2,1)}, u32[]{:S(2)}) copy-start(bf16[8,640]{1,0:T(8,128)(2,1)} %w_ref.1) | copy-start | bytes 30724
  30.6 14.8 %collective-permute-start = (f32[512,640]{1,0:T(8,128)S(1)}, f32[512,640]{1,0:T(8,128)S(1)}, u32[]{:S(2)}, u32[]{:S(2)}) collective-permute-start(f32[512,640]{1,0:T(8,128)S(1)} %get-tuple-element.14), channel_id=1, source_target_pairs={{0,8},{8,0},{1,9},{9,1},{2,10},{10,2},{3,11},{11,3},{4,12},{12,4},... | collective-permute-start | bytes 3932168 | tf_op jit(solution)/shard_map/ppermute | solution.py:158
  104.1 7.1 %collective-permute-start.1 = (bf16[512,640]{1,0:T(8,128)(2,1)S(1)}, bf16[512,640]{1,0:T(8,128)(2,1)S(1)}, u32[]{:S(2)}, u32[]{:S(2)}) collective-permute-start(bf16[512,640]{1,0:T(8,128)(2,1)S(1)} %bitcast.4), channel_id=1, source_target_pairs={{0,8},{8,0},{1,9},{9,1},{2,10},{10,2},{3,11},{11,3},{4,12},{12,4},... | collective-permute-start | bytes 1966088 | tf_op jit(solution)/shard_map/ppermute | solution.py:176

commit v11 on v9

--- a/solution.py
+++ b/solution.py
@@ -42,10 +42,11 @@
     sum_ref[...] = jnp.dot(oth_ref[...], live_ref[...], preferred_element_type=jnp.float32)
 
 
-def own_kernel(own_ref, oth_ref, x_ref, sum_ref, own_back_ref, oth_back_ref):
+def own_kernel(lengths_ref, place_ref, own_ref, oth_ref, x_ref, sum_ref, own_back_ref, oth_back_ref):
     sum_ref[...] = jnp.dot(own_ref[...], x_ref[...], preferred_element_type=jnp.float32)
-    own_back_ref[...] = own_ref[...].T
-    oth_back_ref[...] = oth_ref[...].T
+    live = lax.broadcasted_iota(jnp.int32, own_back_ref.shape, 0) < lengths_ref[place_ref[0]]
+    own_back_ref[...] = jnp.where(live, own_ref[...].T.astype(jnp.float32), 0.0).astype(own_back_ref.dtype)
+    oth_back_ref[...] = jnp.where(live, oth_ref[...].T.astype(jnp.float32), 0.0).astype(oth_back_ref.dtype)
 
 
 def turned_place(k, lines, line):
@@ -104,15 +105,13 @@
     out_ref[...] = jnp.dot(g_ref[...], w_ref[...], preferred_element_type=jnp.float32)
 
 
-def input_kernel(lengths_ref, place_ref, part_ref, g_ref, w_ref, out_ref, held_ref, sems):
-    length = lengths_ref[place_ref[0]]
+def input_kernel(part_ref, g_ref, w_ref, out_ref, held_ref, sems):
     size = out_ref.shape[0] // sems.shape[0]
     copies = []
     for i in range(sems.shape[0]):
         at = slice(i * size, (i + 1) * size)
         total = part_ref[at, :] + jnp.dot(g_ref[at, :], w_ref[...], preferred_element_type=jnp.float32)
-        live = lax.broadcasted_iota(jnp.int32, total.shape, 0) + i * size < length
-        held_ref[at, :] = jnp.where(live, total, 0.0).astype(out_ref.dtype)
+        held_ref[at, :] = total.astype(out_ref.dtype)
         copies.append(pltpu.make_async_copy(held_ref.at[at], out_ref.at[at], sems.at[i]))
         copies[-1].start()
     for copy in copies:
@@ -160,11 +159,11 @@
     mine, own_g, oth_g = call(
         own_kernel,
         [((features, width), jnp.float32), back, back],
-        [VMEM] * 3,
+        [SMEM, SMEM, VMEM, VMEM, VMEM],
         "weight_grads_own",
         flops=work,
         moved=3_000_000,
-    )(own_g, oth_g, live_x)
+    )(lengths, place, own_g, oth_g, live_x)
 
     peers = nz * nx
     (code,) = call(functools.partial(pack_kernel, nx), [((peers, 8, 2 * width + lanes), jnp.int16)], [VMEM] * 3, "pack", moved=4_000_000)(
@@ -184,13 +183,13 @@
     (grad_input,) = call(
         input_kernel,
         [((rows, width), jnp.bfloat16)],
-        [SMEM, SMEM, VMEM, VMEM, VMEM],
+        [VMEM] * 3,
         "input_grads",
         scratch=[pltpu.VMEM((rows, width), w.dtype), pltpu.SemaphoreType.DMA((4,))],
         flops=work,
         moved=4_000_000,
         place=HBM,
-    )(lengths, place, part, oth_g, oth_w)
+    )(part, oth_g, oth_w)
     return (grad_input, grad_weight)
 
 

time: 113 us -> 113 us (level)
  no operation moved by 1% of the time
where the time goes in v11:
time: 113 us
  blocking collectives  85 us (75%)
  starting transfers between devices  17.6 us (16%)
  Pallas kernels  6.52 us (6%)
  waiting for transfers between devices  1.79 us (2%)
    all_to_all x1, blocking collectives, per_device(): code = lax.all_to_all(code, ('x', 'z'), 0, 0)  57.5 us
    all_to_all x1, blocking collectives, per_device(): grads = lax.all_to_all(copies, 'tensor', 0, 0)  27.5 us
    ppermute x1, starting transfers between devices, per_device(): got = lax.ppermute(oth, 'c', swap)  12.2 us
    ppermute x1, starting transfers between devices, per_device(): oth_w = lax.ppermute(own_w, 'c', swap)  5.42 us
  transfers between devices with their start and end apart: 2, of which 2 were waited for; matrix products, arithmetic and copies ran while one was open for 0% of the time, Pallas kernels for 2%

profile of v11, /device:TPU:1, one launch (start us, length us, event | category | flops | bytes accessed | tf_op | source)
XLA Modules:
  0.0 112.5 jit_solution(4023565632655838842)
XLA Ops:
  0.6 0.0 copy-start.1
  0.6 0.9 copy-done.1
  1.5 0.2 sort.1
  1.8 0.0 copy-start
  1.8 0.0 copy-start.3
  1.8 27.5 %all_to_all.10.g_ref = bf16[8,512,128]{2,1,0:T(8,128)(2,1)S(1)} all-to-all(bf16[8,512,128]{2,1,0:T(8,128)(2,1)S(1)} %sort.1), channel_id=1, replica_groups=mesh['z'=8,'x'=8,'c'=2,'tensor'=8] {'tensor'}, dimensions={0} | all-to-all | bytes 2097152 | tf_op jit(solution)/shard_map/all_to_all | solution.py:146
  29.3 0.0 copy-done
  29.3 0.0 copy-done.3
  29.3 0.0 copy-start.2
  29.3 1.3 %weight_grads_other.1 = (f32[512,640]{1,0:T(8,128)S(1)}, bf16[512,512]{1,0:T(8,128)(2,1)S(1)}, bf16[512,512]{1,0:T(8,128)(2,1)S(1)}, bf16[512,640]{1,0:T(8,128)(2,1)S(1)}) custom-call(s32[128]{0:T(128)S(1)} %copy-done.3, s32[1]{0:T(128)} %bitcast.place_ref, bf16[8,512,128]{2,1,0:T(8,128)(2,1)S(1)} %all_to_all.10.g_ref, bf16[512,640]{1,0:T(8,128)(2,1)S(1)} %copy-done), custom_call_target="tpu_custom_call" | custom-call | flops 335544320 | bytes 3000000 | tf_op jit(solution)/shard_map/weight_grads_other/pallas_call | solution.py:149
  30.6 12.2 %collective-permute-start = (f32[512,640]{1,0:T(8,128)S(1)}, f32[512,640]{1,0:T(8,128)S(1)}, u32[]{:S(2)}, u32[]{:S(2)}) collective-permute-start(f32[512,640]{1,0:T(8,128)S(1)} %get-tuple-element.14), channel_id=1, source_target_pairs={{0,8},{8,0},{1,9},{9,1},{2,10},{10,2},{3,11},{11,3},{4,12},{12,4},... | collective-permute-start | bytes 3932168 | tf_op jit(solution)/shard_map/ppermute | solution.py:157
  42.8 1.1 %weight_grads_own.1 = (f32[512,640]{1,0:T(8,128)S(1)}, bf16[512,512]{1,0:T(8,128)(2,1)S(1)}, bf16[512,512]{1,0:T(8,128)(2,1)S(1)}) custom-call(s32[128]{0:T(128)S(1)} %copy-done.3, s32[1]{0:T(128)} %bitcast.place_ref, bf16[512,512]{1,0:T(8,128)(2,1)S(1)} %get-tuple-element.9.own_ref, bf16[512,512]{1,0:T(8,128)(2,1)S(1)} %get-tuple-element.10.oth_ref, ...), custom_call_target="tpu_custom_call" | custom-call | flops 335544320 | bytes 3000000 | tf_op jit(solution)/shard_map/weight_grads_own/pallas_call | solution.py:159
  43.9 1.5 %collective-permute-done = f32[512,640]{1,0:T(8,128)S(1)} collective-permute-done((f32[512,640]{1,0:T(8,128)S(1)}, f32[512,640]{1,0:T(8,128)S(1)}, u32[]{:S(2)}, u32[]{:S(2)}) %collective-permute-start) | collective-permute-done | bytes 1310752 | tf_op jit(solution)/shard_map/ppermute | solution.py:157
  45.4 0.0 copy-done.2
  45.4 0.4 pack.1
  45.8 57.5 %all_to_all.11.in_ref = s16[64,8,1408]{2,1,0:T(8,128)(2,1)S(1)} all-to-all(s16[64,8,1408]{2,1,0:T(8,128)(2,1)S(1)} %pack.1), channel_id=1, replica_groups=mesh['z'=8,'x'=8,'c'=2,'tensor'=8] {'x','z'}, dimensions={0} | all-to-all | bytes 2883584 | tf_op jit(solution)/shard_map/all_to_all | solution.py:172
  103.3 0.7 unpack_weights.1
  104.1 5.4 %collective-permute-start.1 = (bf16[512,640]{1,0:T(8,128)(2,1)S(1)}, bf16[512,640]{1,0:T(8,128)(2,1)S(1)}, u32[]{:S(2)}, u32[]{:S(2)}) collective-permute-start(bf16[512,640]{1,0:T(8,128)(2,1)S(1)} %bitcast.4), channel_id=1, source_target_pairs={{0,8},{8,0},{1,9},{9,1},{2,10},{10,2},{3,11},{11,3},{4,12},{12,4},... | collective-permute-start | bytes 1966088 | tf_op jit(solution)/shard_map/ppermute | solution.py:175
  109.5 0.8 unpack_sum.1
  110.4 0.6 input_grads_own.1.part_ref
  110.9 0.3 collective-permute-done.1.w_ref
  111.2 1.3 %input_grads.1 = bf16[512,640]{1,0:T(8,128)(2,1)} custom-call(f32[512,640]{1,0:T(8,128)S(1)} %input_grads_own.1.part_ref, bf16[512,512]{1,0:T(8,128)(2,1)S(1)} %get-tuple-element.15.g_ref, bf16[512,640]{1,0:T(8,128)(2,1)S(1)} %collective-permute-done.1.w_ref), custom_call_target="tpu_custom_call" | custom-call | flops 335544320 | bytes 4000000 | tf_op jit(solution)/shard_map/input_grads/pallas_call | solution.py:183
Async XLA Ops:
  0.6 0.9 copy-start.1
  1.8 27.5 %copy-start = (bf16[512,640]{1,0:T(8,128)(2,1)S(1)}, bf16[512,640]{1,0:T(8,128)(2,1)}, u32[]{:S(2)}) copy-start(bf16[512,640]{1,0:T(8,128)(2,1)} %x_ref.1) | copy-start | bytes 1966084
  1.8 27.5 %copy-start.3 = (s32[128]{0:T(128)S(1)}, s32[128]{0:T(128)}, u32[]{:S(2)}) copy-start(s32[128]{0:T(128)} %lengths_ref.3) | copy-start | bytes 1540
  29.3 16.1 %copy-start.2 = (bf16[8,640]{1,0:T(8,128)(2,1)S(1)}, bf16[8,640]{1,0:T(8,128)(2,1)}, u32[]{:S(2)}) copy-start(bf16[8,640]{1,0:T(8,128)(2,1)} %w_ref.1) | copy-start | bytes 30724
  30.6 14.8 %collective-permute-start = (f32[512,640]{1,0:T(8,128)S(1)}, f32[512,640]{1,0:T(8,128)S(1)}, u32[]{:S(2)}, u32[]{:S(2)}) collective-permute-start(f32[512,640]{1,0:T(8,128)S(1)} %get-tuple-element.14), channel_id=1, source_target_pairs={{0,8},{8,0},{1,9},{9,1},{2,10},{10,2},{3,11},{11,3},{4,12},{12,4},... | collective-permute-start | bytes 3932168 | tf_op jit(solution)/shard_map/ppermute | solution.py:157
  104.1 7.1 %collective-permute-start.1 = (bf16[512,640]{1,0:T(8,128)(2,1)S(1)}, bf16[512,640]{1,0:T(8,128)(2,1)S(1)}, u32[]{:S(2)}, u32[]{:S(2)}) collective-permute-start(bf16[512,640]{1,0:T(8,128)(2,1)S(1)} %bitcast.4), channel_id=1, source_target_pairs={{0,8},{8,0},{1,9},{9,1},{2,10},{10,2},{3,11},{11,3},{4,12},{12,4},... | collective-permute-start | bytes 1966088 | tf_op jit(solution)/shard_map/ppermute | solution.py:175
